TPU v7x, 32 devices: a whole 2x2x4 slice. The times are simulated.
32 devices in a mesh: expert: 16 (over z, y, x), tensor: 2 (over core).
Axes of the slice: x: 2, y: 2, z: 4, core: 2. Of those that a mesh axis runs over, the one named last changes fastest.
Arguments:
- attn_parts: bfloat16 [2, 2048, 4096], P('tensor', 'expert'), may hold values from -4 to 4
- resid: bfloat16 [2048, 4096], P('expert', 'tensor'), may hold values from -48 to 48
- norm_gain: float32 [4096], P('tensor'), may hold values from 0.1 to 1.9
- w_gate: bfloat16 [16, 4096, 768], P('expert', 'tensor'), may hold values from -0.09375 to 0.09375
- w_up: bfloat16 [16, 4096, 768], P('expert', 'tensor'), may hold values from -0.09375 to 0.09375
- w_down: bfloat16 [16, 768, 4096], P('expert', None, 'tensor'), may hold values from -0.21875 to 0.21875
- expert_ids: int32 [2048, 4], P('expert'), may hold values from 0 to 15, all different within a row; in each aligned block of 128 rows (0 to 127, 128 to 255, ...) at most 40 rows name the same one
- gate_weights: float32 [2048, 4], P('expert'), may hold values from 0.1 to 1
- grad_out: bfloat16 [2048, 4096], P('expert', 'tensor'), may hold values from -6 to 6
Outputs:
- output: bfloat16 [2048, 4096], P('expert', 'tensor')
- grad_input: bfloat16 [2048, 4096], P('expert', 'tensor')
Inputs may be any that keep to these rules, and one draw needn't show every extreme that they name: `expert_ids`: each row names 4 different experts. In each aligned block of 128 rows (the tokens of one group) no expert is named by more than 40 rows, a bound that some block reaches.
All inputs are finite; a program needn't handle non-finite values.
Results may differ from a plain program's by a relative error of at most 0.014.
Values may be sent and summed in bfloat16 or wider, within the bound.
A program may use at most 128 MiB of HBM per device.

v0:
```python
import jax
import jax.numpy as jnp
from jax import lax
from jax.sharding import PartitionSpec as P

D = 4096


epsilon = 1e-06


def route_tables(expert_ids, gate_weights, experts, capacity):
    pairs = expert_ids.reshape(-1)
    pair_count = pairs.shape[0]
    expert_hot = (pairs[:, None] == jnp.arange(experts, dtype=jnp.int32)[None, :]).astype(jnp.int32)
    earlier = jnp.cumsum(expert_hot, axis=0) - expert_hot
    position = jnp.sum(earlier * expert_hot, axis=1)
    slot_index = pairs * capacity + position
    slot_hot = (
        slot_index[:, None] == jnp.arange(experts * capacity, dtype=jnp.int32)[None, :]
    ).astype(jnp.float32)
    owner = jnp.arange(pair_count, dtype=jnp.int32) // expert_ids.shape[1]
    token_hot = (
        owner[:, None] == jnp.arange(expert_ids.shape[0], dtype=jnp.int32)[None, :]
    ).astype(jnp.float32)
    dispatch = jnp.dot(slot_hot.T, token_hot, precision=lax.Precision.HIGHEST)
    slot_gate = jnp.sum(slot_hot * gate_weights.reshape(-1)[:, None], axis=0)
    return (dispatch, slot_index.reshape(expert_ids.shape), slot_gate)


def row_sums(values):
    return lax.psum(jnp.sum(values, axis=1), "tensor")


def to_owner(blocks):
    return lax.all_to_all(blocks, "expert", split_axis=0, concat_axis=0, tiled=True)


def to_source(blocks):
    return lax.all_to_all(blocks, "expert", split_axis=0, concat_axis=0, tiled=True)


def swish_forward(gate_pre, up_pre):
    return (jax.nn.silu(gate_pre) * up_pre).astype(jnp.bfloat16)


def swish_back(grad_act, gate_pre, up_pre):
    sigmoid_gate = jax.nn.sigmoid(gate_pre)
    grad_gate = grad_act * up_pre * sigmoid_gate * (1.0 + gate_pre * (1.0 - sigmoid_gate))
    grad_up = grad_act * jax.nn.silu(gate_pre)
    return (grad_gate.astype(jnp.bfloat16), grad_up.astype(jnp.bfloat16))


def body(attn_parts, resid, norm_gain, w_gate, w_up, w_down, expert_ids, gate_weights, grad_out):
    experts = lax.axis_size("expert")
    tokens_here = expert_ids.shape[0]
    capacity = 5 * tokens_here * expert_ids.shape[1] // (4 * experts)
    feature_width = resid.shape[1]
    attention = lax.psum_scatter(
        attn_parts[0].astype(jnp.float32).astype(jnp.bfloat16),
        "tensor",
        scatter_dimension=1,
        tiled=True,
    ).astype(jnp.float32)
    hidden_in = resid.astype(jnp.float32) + attention
    inv_rms = lax.rsqrt(row_sums(hidden_in * hidden_in) / D + epsilon)
    normed = (hidden_in * inv_rms[:, None] * norm_gain[None, :]).astype(jnp.bfloat16)
    dispatch, slot_index, slot_gate = route_tables(expert_ids, gate_weights, experts, capacity)
    dispatch_half = dispatch.astype(jnp.bfloat16)
    sent = jnp.dot(dispatch_half, normed, preferred_element_type=jnp.float32).astype(jnp.bfloat16)
    rows = to_owner(sent.reshape(experts, capacity, feature_width)).reshape(
        experts * capacity, feature_width
    )
    gate_part = jnp.dot(rows, w_gate[0], preferred_element_type=jnp.float32)
    up_part = jnp.dot(rows, w_up[0], preferred_element_type=jnp.float32)
    gate_pre, up_pre = (
        lax.psum(gate_part.astype(jnp.bfloat16), "tensor").astype(jnp.float32),
        lax.psum(up_part.astype(jnp.bfloat16), "tensor").astype(jnp.float32),
    )
    activation = swish_forward(gate_pre, up_pre)
    expert_out = jnp.dot(activation, w_down[0], preferred_element_type=jnp.float32).astype(
        jnp.bfloat16
    )
    returned = to_source(expert_out.reshape(experts, capacity, feature_width)).reshape(
        -1, feature_width
    )
    picked = jnp.take(returned, slot_index.reshape(-1), axis=0).reshape(
        tokens_here, -1, feature_width
    )
    moe = jnp.sum(gate_weights[:, :, None] * picked.astype(jnp.float32), axis=1)
    output = (hidden_in + moe).astype(jnp.bfloat16)
    upstream = grad_out.astype(jnp.float32)
    copied = jnp.dot(dispatch_half, grad_out, preferred_element_type=jnp.float32)
    grad_slots = (copied * slot_gate[:, None]).astype(jnp.bfloat16)
    grad_arrived = to_owner(grad_slots.reshape(experts, capacity, feature_width)).reshape(
        -1, feature_width
    )
    grad_part = jnp.dot(grad_arrived, w_down[0].T, preferred_element_type=jnp.float32)
    grad_act = lax.psum(grad_part.astype(jnp.bfloat16), "tensor").astype(jnp.float32)
    grad_gate, grad_up = swish_back(grad_act, gate_pre, up_pre)
    grad_expert = (
        jnp.dot(grad_gate, w_gate[0].T, preferred_element_type=jnp.float32)
        + jnp.dot(grad_up, w_up[0].T, preferred_element_type=jnp.float32)
    ).astype(jnp.bfloat16)
    grad_back = to_source(grad_expert.reshape(experts, capacity, feature_width))
    grad_normed = jnp.dot(
        dispatch_half.T, grad_back.reshape(-1, feature_width), preferred_element_type=jnp.float32
    )
    scaled = grad_normed * norm_gain[None, :]
    inner = row_sums(hidden_in * scaled)
    grad_input = (
        upstream + inv_rms[:, None] * scaled - hidden_in * (inv_rms**3 * inner / D)[:, None]
    )
    return (output, grad_input.astype(jnp.bfloat16))


def solution(mesh):
    return jax.shard_map(
        body,
        mesh=mesh,
        in_specs=(
            P("tensor", "expert", None),
            P("expert", "tensor"),
            P("tensor"),
            P("expert", "tensor", None),
            P("expert", "tensor", None),
            P("expert", None, "tensor"),
            P("expert", None),
            P("expert", None),
            P("expert", "tensor"),
        ),
        out_specs=(P("expert", "tensor"), P("expert", "tensor")),
        check_vma=False,
    )
```

profile of v0, /device:TPU:17, one launch (start us, length us, event | category | flops | bytes accessed | tf_op | source)
XLA Modules:
  0.0 335.4 jit_solution(15030270844587692438)
XLA Ops:
  7.2 0.0 copy-start
  7.2 0.9 copy.26
  8.1 0.1 reshape.114
  8.2 0.1 eq.52
  8.3 0.8 copy.25
  9.1 0.1 mul.138
  9.2 1.2 reduce-window.6
  10.4 0.2 slice_reduce_fusion
  10.7 0.1 fusion.40
  10.8 0.2 select_reduce_fusion
  11.0 0.7 fusion.29
  11.7 3.4 %multiply_convert_fusion = bf16[640,2048]{1,0:T(8,128)(2,1)} fusion(bf16[640,128]{1,0:T(8,128)(2,1)S(1)} %fusion.29, bf16[128,2048]{1,0:T(8,128)(2,1)} %param.17, f32[640]{0:T(1024)S(1)} %select_reduce_fusion), kind=kOutput, calls=%fused_computation.2 | convolution fusion | flops 338165760 | bytes 3312128 | tf_op jit(solution)/shard_map/dot_general | solution.py:93
  15.1 0.0 copy-start.5
  15.1 6.7 %all-to-all-start.2 = ((bf16[16,40,2048]{2,1,0:T(8,128)(2,1)}), bf16[16,40,2048]{2,1,0:T(8,128)(2,1)}, u32[]{:S(2)}, u32[]{:S(2)}) async-start(bf16[16,40,2048]{2,1,0:T(8,128)(2,1)} %bitcast.59), calls=%async_computation.3 | async-start | bytes 5242880 | tf_op jit(solution)/shard_map/all_to_all | solution.py:36
  21.8 0.0 reduce-scatter.2.cloned.1.call-start
  21.8 0.7 reduce-scatter.2.cloned.1.call-update
  22.5 13.1 %reduce-scatter.2.cloned.1.call-done = bf16[128,2048]{1,0:T(8,128)(2,1)} async-done(((bf16[128,4096]{1,0:T(8,128)(2,1)}), bf16[128,2048]{1,0:T(8,128)(2,1)}) %reduce-scatter.2.cloned.1.call-update) | async-done | bytes 524304 | tf_op jit(solution)/shard_map/reduce_scatter | solution.py:59
  35.6 1.5 multiply_reduce_fusion.2
  37.0 2.5 psum.35
  39.5 0.0 copy-done.5
  39.5 3.6 %convolution_convert_fusion.1 = bf16[640,2048]{1,0:T(8,128)(2,1)} fusion(bf16[640,128]{1,0:T(8,128)(2,1)S(1)} %fusion.29, bf16[128,2048]{1,0:T(8,128)(2,1)} %reduce-scatter.2.cloned.1.call-done, bf16[128,2048]{1,0:T(8,128)(2,1)} %param.10, f32[2048]{0:T(1024)S(1)} %copy-done.5, f32[128]{0:T(128)S(1)} %add_rsqrt_fusion), kind=kOutput, calls=%fused_computation.5 | convolution fusion | flops 338427904 | bytes 3842560 | tf_op jit(solution)/shard_map/dot_general | solution.py:70
  43.1 37.3 %all-to-all-done.2 = bf16[16,40,2048]{2,1,0:T(8,128)(2,1)} async-done(((bf16[16,40,2048]{2,1,0:T(8,128)(2,1)}), bf16[16,40,2048]{2,1,0:T(8,128)(2,1)}, u32[]{:S(2)}, u32[]{:S(2)}) %all-to-all-start.2) | async-done | bytes 2621472 | tf_op jit(solution)/shard_map/all_to_all | solution.py:36
  80.4 5.0 %all-to-all-start = ((bf16[16,40,2048]{2,1,0:T(8,128)(2,1)}), bf16[16,40,2048]{2,1,0:T(8,128)(2,1)}, u32[]{:S(2)}, u32[]{:S(2)}) async-start(bf16[16,40,2048]{2,1,0:T(8,128)(2,1)} %bitcast.60), calls=%async_computation.1 | async-start | bytes 5242880 | tf_op jit(solution)/shard_map/all_to_all | solution.py:36
  85.4 0.0 all-reduce.3.cloned.1.call-start
  85.5 0.0 copy-done
  85.5 5.0 %fusion.25 = bf16[640,768]{1,0:T(8,128)(2,1)} fusion(bf16[640,2048]{1,0:T(8,128)(2,1)} %bitcast.12, bf16[1,768,2048]{2,1,0:T(8,128)(2,1)S(1)} %copy-done), kind=kOutput, calls=%fused_computation.34 | convolution fusion | flops 2013757440 | bytes 6750208 | tf_op jit(solution)/shard_map/dot_general | solution.py:98
  90.5 52.7 %all-to-all-done = bf16[16,40,2048]{2,1,0:T(8,128)(2,1)} async-done(((bf16[16,40,2048]{2,1,0:T(8,128)(2,1)}), bf16[16,40,2048]{2,1,0:T(8,128)(2,1)}, u32[]{:S(2)}, u32[]{:S(2)}) %all-to-all-start) | async-done | bytes 2621472 | tf_op jit(solution)/shard_map/all_to_all | solution.py:36
  143.2 0.0 copy-start.7
  143.2 6.0 %fusion.22 = bf16[640,768]{1,0:T(8,128)(2,1)} fusion(bf16[640,2048]{1,0:T(8,128)(2,1)} %bitcast.3, bf16[1,2048,768]{2,1,0:T(8,128)(2,1)} %param.13), kind=kOutput, calls=%fused_computation.33 | convolution fusion | flops 2013757440 | bytes 6750208 | tf_op jit(solution)/shard_map/dot_general | solution.py:75
  149.2 0.0 copy-done.7
  149.2 4.9 %fusion.19 = bf16[640,768]{1,0:T(8,128)(2,1)} fusion(bf16[640,2048]{1,0:T(8,128)(2,1)} %bitcast.3, bf16[1,2048,768]{2,1,0:T(8,128)(2,1)S(1)} %copy-done.7), kind=kOutput, calls=%fused_computation.32 | convolution fusion | flops 2013757440 | bytes 6750208 | tf_op jit(solution)/shard_map/dot_general | solution.py:74
  154.1 0.0 all-reduce.3.cloned.1.call-update
  154.1 25.0 %all-reduce.3.cloned.1.call-done = (bf16[640,768]{1,0:T(8,128)(2,1)}, bf16[640,768]{1,0:T(8,128)(2,1)}, bf16[640,768]{1,0:T(8,128)(2,1)}) async-done(((bf16[640,768]{1,0:T(8,128)(2,1)}, bf16[640,768]{1,0:T(8,128)(2,1)}, bf16[640,768]{1,0:T(8,128)(2,1)}), (bf16[640,768]{1,0:T(8,128)(2,1)}, bf16[640,768]{1,0:T(8,128)(2,1)}, bf16[640,768]{1,0:T(8,128)(2,1)})) %all-reduce.3.cloned.1.call-update) | async-done | bytes 2949136 | tf_op jit(solution)/shard_map/psum | solution.py:78
  179.1 5.4 %convolution_convert_fusion = bf16[640,2048]{1,0:T(8,128)(2,1)} fusion(bf16[1,768,2048]{2,1,0:T(8,128)(2,1)S(1)} %copy-done, bf16[640,768]{1,0:T(8,128)(2,1)} %get-tuple-element.2, bf16[640,768]{1,0:T(8,128)(2,1)} %get-tuple-element.3), kind=kOutput, calls=%fused_computation.4 | convolution fusion | flops 2018508800 | bytes 7733248 | tf_op jit(solution)/shard_map/dot_general | solution.py:81
  184.5 6.4 %all-to-all-start.1 = ((bf16[16,40,2048]{2,1,0:T(8,128)(2,1)}), bf16[16,40,2048]{2,1,0:T(8,128)(2,1)}, u32[]{:S(2)}, u32[]{:S(2)}) async-start(bf16[16,40,2048]{2,1,0:T(8,128)(2,1)} %bitcast.62), calls=%async_computation.2 | async-start | bytes 5242880 | tf_op jit(solution)/shard_map/all_to_all | solution.py:40
  190.8 0.0 copy-start.8
  190.9 0.0 copy-start.9
  190.9 0.0 copy-start.10
  190.9 5.6 %fusion.6 = f32[640,2048]{1,0:T(8,128)S(1)} fusion(bf16[1,2048,768]{2,1,0:T(8,128)(2,1)} %param.12, bf16[640,768]{1,0:T(8,128)(2,1)} %get-tuple-element.2, bf16[640,768]{1,0:T(8,128)(2,1)} %get-tuple-element.4, bf16[640,768]{1,0:T(8,128)(2,1)} %get-tuple-element.3), kind=kOutput, calls=%fused_computation.12 | convolution fusion | flops 2019655680 | bytes 11337728 | tf_op jit(solution)/shard_map/dot_general | solution.py:102
  196.4 0.0 copy-done.8
  196.5 0.0 copy-done.9
  196.5 0.0 copy-done.10
  196.5 3.9 %add_convert_fusion = bf16[640,2048]{1,0:T(8,128)(2,1)} fusion(f32[640,2048]{1,0:T(8,128)S(1)} %fusion.6, bf16[1,2048,768]{2,1,0:T(8,128)(2,1)S(1)} %copy-done.8, bf16[640,768]{1,0:T(8,128)(2,1)S(1)} %copy-done.10, bf16[640,768]{1,0:T(8,128)(2,1)S(1)} %copy-done.9), kind=kOutput, calls=%fused_computation.1 | convolution fusion | flops 2019819520 | bytes 12976128 | tf_op jit(solution)/shard_map/dot_general | solution.py:103
  200.4 49.4 %all-to-all-done.1 = bf16[16,40,2048]{2,1,0:T(8,128)(2,1)} async-done(((bf16[16,40,2048]{2,1,0:T(8,128)(2,1)}), bf16[16,40,2048]{2,1,0:T(8,128)(2,1)}, u32[]{:S(2)}, u32[]{:S(2)}) %all-to-all-start.1) | async-done | bytes 2621472 | tf_op jit(solution)/shard_map/all_to_all | solution.py:40
  249.7 0.0 copy-start.6
  249.7 5.5 %all-to-all-start.3 = ((bf16[16,40,2048]{2,1,0:T(8,128)(2,1)}), bf16[16,40,2048]{2,1,0:T(8,128)(2,1)}, u32[]{:S(2)}, u32[]{:S(2)}) async-start(bf16[16,40,2048]{2,1,0:T(8,128)(2,1)} %bitcast.61), calls=%async_computation.4 | async-start | bytes 5242880 | tf_op jit(solution)/shard_map/all_to_all | solution.py:40
  255.2 0.1 reduce_sum.50
  255.3 0.0 copy-done.6
  255.4 0.1 copy.31
  255.5 0.1 mul.136
  255.6 0.1 copy.29
  255.7 0.1 copy.30
  255.9 7.4 %gather_fusion = bf16[512,2048]{1,0:T(8,128)(2,1)} fusion(bf16[640,2048]{1,0:T(8,128)(2,1)} %bitcast.8, s32[1024]{0:T(1024)S(1)} %pad_clamp_fusion), kind=kCustom, calls=%fused_computation | custom fusion | bytes 4196352 | tf_op jit(solution)/shard_map/jit(_take)/gather | solution.py:87
  263.2 4.1 %gather.7 = bf16[128,4,2048]{2,1,0:T(4,128)(2,1)} reshape(bf16[512,2048]{1,0:T(8,128)(2,1)} %gather_fusion) | data formatting | bytes 4194304 | tf_op jit(solution)/shard_map/jit(_take)/gather | solution.py:87
  267.3 45.6 %all-to-all-done.3 = bf16[16,40,2048]{2,1,0:T(8,128)(2,1)} async-done(((bf16[16,40,2048]{2,1,0:T(8,128)(2,1)}), bf16[16,40,2048]{2,1,0:T(8,128)(2,1)}, u32[]{:S(2)}, u32[]{:S(2)}) %all-to-all-start.3) | async-done | bytes 2621472 | tf_op jit(solution)/shard_map/all_to_all | solution.py:40
  313.0 3.6 %multiply_reduce_fusion.1 = (f32[128]{0:T(128)S(1)}, f32[128,2048]{1,0:T(8,128)}) fusion(bf16[128,2048]{1,0:T(8,128)(2,1)} %reduce-scatter.2.cloned.1.call-done, bf16[128,2048]{1,0:T(8,128)(2,1)} %param.10, f32[2048]{0:T(1024)S(1)} %copy-done.5, bf16[640,128]{1,0:T(8,128)(2,1)S(1)} %fusion.29, bf16[640,2048]{1,0:T(8,128)(2,1)} %bitcast.14), kind=kOutput, calls=%fused_computation.40 | convolution fusion | flops 337117056 | bytes 4891136 | tf_op jit(solution)/shard_map/dot_general | solution.py:106
  316.6 4.7 %psum.39 = f32[128]{0:T(128)S(1)} all-reduce(f32[128]{0:T(128)S(1)} %get-tuple-element.7), channel_id=1, replica_groups=mesh['expert'=16,'tensor'=2] {'tensor'}, use_global_device_ids=true, to_apply=%region_12.13 | all-reduce | flops 128 | bytes 1024 | tf_op jit(solution)/shard_map/psum | solution.py:32
  321.3 0.0 copy-start.1
  321.3 5.8 %multiply_reduce_fusion = f32[128,2048]{1,0:T(8,128)S(1)} fusion(bf16[128,4,2048]{2,1,0:T(4,128)(2,1)} %gather.7, f32[128,4]{1,0:T(8,128)S(1)} %copy.25, pred[128,4]{1,0:T(8,128)(4,1)S(1)} %copy.30), kind=kLoop, calls=%fused_computation.3 | loop fusion | flops 3932160 | bytes 3148288 | tf_op jit(solution)/shard_map/reduce_sum | solution.py:90
  327.2 0.0 copy-done.1
  327.2 0.0 copy-done.2
  327.2 0.0 copy-done.3
  327.2 0.0 copy-done.4
  327.2 1.4 subtract_convert_fusion
  (13 shorter events, 0.1 us)
Async XLA Ops:
  7.2 78.3 %copy-start = (bf16[1,768,2048]{2,1,0:T(8,128)(2,1)S(1)}, bf16[1,768,2048]{2,1,0:T(8,128)(2,1)}, u32[]{:S(2)}) copy-start(bf16[1,768,2048]{2,1,0:T(8,128)(2,1)} %param.14) | copy-start | bytes 9437188
  15.1 24.4 %copy-start.5 = (f32[2048]{0:T(1024)S(1)}, f32[2048]{0:T(1024)}, u32[]{:S(2)}) copy-start(f32[2048]{0:T(1024)} %param.11) | copy-start | bytes 24580
  15.1 65.3 %all-to-all-start.2 = ((bf16[16,40,2048]{2,1,0:T(8,128)(2,1)}), bf16[16,40,2048]{2,1,0:T(8,128)(2,1)}, u32[]{:S(2)}, u32[]{:S(2)}) async-start(bf16[16,40,2048]{2,1,0:T(8,128)(2,1)} %bitcast.59), calls=%async_computation.3 | async-start | bytes 5242880 | tf_op jit(solution)/shard_map/all_to_all | solution.py:36
  21.8 13.8 %reduce-scatter.2.cloned.1.call-start = ((), (), s32[]{:S(2)}) async-start(), calls=%async_computation.5 | async-start | bytes 1572864 | tf_op jit(solution)/shard_map/reduce_scatter | solution.py:59
  80.4 62.8 %all-to-all-start = ((bf16[16,40,2048]{2,1,0:T(8,128)(2,1)}), bf16[16,40,2048]{2,1,0:T(8,128)(2,1)}, u32[]{:S(2)}, u32[]{:S(2)}) async-start(bf16[16,40,2048]{2,1,0:T(8,128)(2,1)} %bitcast.60), calls=%async_computation.1 | async-start | bytes 5242880 | tf_op jit(solution)/shard_map/all_to_all | solution.py:36
  85.4 93.6 %all-reduce.3.cloned.1.call-start = ((), (), s32[]{:S(2)}) async-start(), calls=%async_computation.6 | async-start | bytes 5898240 | tf_op jit(solution)/shard_map/psum | solution.py:78
  143.2 6.0 %copy-start.7 = (bf16[1,2048,768]{2,1,0:T(8,128)(2,1)S(1)}, bf16[1,2048,768]{2,1,0:T(8,128)(2,1)}, u32[]{:S(2)}) copy-start(bf16[1,2048,768]{2,1,0:T(8,128)(2,1)} %param.12) | copy-start | bytes 9437188
  184.5 65.3 %all-to-all-start.1 = ((bf16[16,40,2048]{2,1,0:T(8,128)(2,1)}), bf16[16,40,2048]{2,1,0:T(8,128)(2,1)}, u32[]{:S(2)}, u32[]{:S(2)}) async-start(bf16[16,40,2048]{2,1,0:T(8,128)(2,1)} %bitcast.62), calls=%async_computation.2 | async-start | bytes 5242880 | tf_op jit(solution)/shard_map/all_to_all | solution.py:40
  190.8 5.6 %copy-start.8 = (bf16[1,2048,768]{2,1,0:T(8,128)(2,1)S(1)}, bf16[1,2048,768]{2,1,0:T(8,128)(2,1)}, u32[]{:S(2)}) copy-start(bf16[1,2048,768]{2,1,0:T(8,128)(2,1)} %param.13) | copy-start | bytes 9437188
  190.9 5.6 %copy-start.9 = (bf16[640,768]{1,0:T(8,128)(2,1)S(1)}, bf16[640,768]{1,0:T(8,128)(2,1)}, u32[]{:S(2)}) copy-start(bf16[640,768]{1,0:T(8,128)(2,1)} %get-tuple-element.3) | copy-start | bytes 2949124
  190.9 5.6 %copy-start.10 = (bf16[640,768]{1,0:T(8,128)(2,1)S(1)}, bf16[640,768]{1,0:T(8,128)(2,1)}, u32[]{:S(2)}) copy-start(bf16[640,768]{1,0:T(8,128)(2,1)} %get-tuple-element.4) | copy-start | bytes 2949124
  249.7 5.6 %copy-start.6 = (s32[128,4]{0,1:T(4,128)S(1)}, s32[128,4]{0,1:T(4,128)}, u32[]{:S(2)}) copy-start(s32[128,4]{0,1:T(4,128)} %param.15) | copy-start | bytes 6148
  249.7 63.3 %all-to-all-start.3 = ((bf16[16,40,2048]{2,1,0:T(8,128)(2,1)}), bf16[16,40,2048]{2,1,0:T(8,128)(2,1)}, u32[]{:S(2)}, u32[]{:S(2)}) async-start(bf16[16,40,2048]{2,1,0:T(8,128)(2,1)} %bitcast.61), calls=%async_computation.4 | async-start | bytes 5242880 | tf_op jit(solution)/shard_map/all_to_all | solution.py:40
  321.3 5.8 %copy-start.1 = (bf16[128,2048]{1,0:T(8,128)(2,1)S(1)}, bf16[128,2048]{1,0:T(8,128)(2,1)}, u32[]{:S(2)}) copy-start(bf16[128,2048]{1,0:T(8,128)(2,1)} %param.10) | copy-start | bytes 1572868
  321.3 5.8 %copy-start.2 = (bf16[128,2048]{1,0:T(8,128)(2,1)S(1)}, bf16[128,2048]{1,0:T(8,128)(2,1)}, u32[]{:S(2)}) copy-start(bf16[128,2048]{1,0:T(8,128)(2,1)} %reduce-scatter.2.cloned.1.call-done) | copy-start | bytes 1572868
  321.3 5.9 %copy-start.3 = (f32[128,2048]{1,0:T(8,128)S(1)}, f32[128,2048]{1,0:T(8,128)}, u32[]{:S(2)}) copy-start(f32[128,2048]{1,0:T(8,128)} %get-tuple-element.8) | copy-start | bytes 3145732
  321.3 5.9 %copy-start.4 = (bf16[128,2048]{1,0:T(8,128)(2,1)S(1)}, bf16[128,2048]{1,0:T(8,128)(2,1)}, u32[]{:S(2)}) copy-start(bf16[128,2048]{1,0:T(8,128)(2,1)} %param.17) | copy-start | bytes 1572868
Sparse Core Ops, SparseCore 0:
  24.8 10.6 reduce-scatter.1
  154.2 24.7 all-reduce.2
where the time goes:
time: 337 us; the launch traced here: 335 us
  waiting for transfers between devices  224 us (66%)
  matrix products  42.1 us (12%)
  starting transfers between devices  23.7 us (7%)
  local copies, waits for them, and re-layouts  14.3 us (4%)
  between operations  14.3 us (4%)
  other arithmetic  10.2 us (3%)
  blocking collectives  7.18 us (2%)
    all_to_all x2, waiting for transfers between devices, to_source(): lax.all_to_all(blocks, 'expert', split_axis=0, concat_axis=0, tiled=True)  95 us
    all_to_all x2, waiting for transfers between devices, to_owner(): lax.all_to_all(blocks, 'expert', split_axis=0, concat_axis=0, tiled=True)  89.9 us
    psum x1, waiting for transfers between devices, body(): lax.psum(up_part.astype(jnp.bfloat16), 'tensor').astype(jnp.float32)  25 us
    reduce_scatter x1, waiting for transfers between devices, body(): lax.psum_scatter(attn_parts[0].astype(jnp.float32).astype(jnp.bfloat16),...  13.1 us
    all_to_all x2, starting transfers between devices, to_source(): lax.all_to_all(blocks, 'expert', split_axis=0, concat_axis=0, tiled=True)  11.9 us
    all_to_all x2, starting transfers between devices, to_owner(): lax.all_to_all(blocks, 'expert', split_axis=0, concat_axis=0, tiled=True)  11.7 us
    gather x2, local copies, waits for them, and re-layouts, body(): jnp.take(returned, slot_index.reshape(-1), axis=0)  11.5 us
    psum x2, blocking collectives, row_sums(): return lax.psum(jnp.sum(values, axis=1), 'tensor')  7.18 us
  transfers between devices with their start and end apart: 6, of which 6 were waited for; matrix products, arithmetic and copies ran while one was open for 9% of the time, Pallas kernels for 0%

commit v1 on v0

v1 whole, which is shorter than its diff:
```python
import functools

import jax
import jax.numpy as jnp
from jax import lax
from jax.experimental import pallas as pl
from jax.experimental.pallas import tpu as pltpu
from jax.sharding import PartitionSpec as P

D = 4096
Z = 4
MESH = pl.DeviceIdType.MESH
COLUMNS = 512

epsilon = 1e-06


def device(expert):
    return (expert, lax.axis_index("tensor"))


def position(plane):
    me = lax.axis_index("expert")
    return me, me // plane, me % plane


def greet(plane):
    me, z, p = position(plane)
    barrier = pltpu.get_barrier_semaphore()

    def hello(d, carry):
        pl.semaphore_signal(
            barrier, inc=1, device_id=device(z * plane + (p + d) % plane), device_id_type=MESH
        )
        return carry

    lax.fori_loop(1, plane, hello, 0)

    @pl.when(z > 0)
    def _():
        pl.semaphore_signal(barrier, inc=1, device_id=device(me - plane), device_id_type=MESH)

    @pl.when(z < Z - 1)
    def _():
        pl.semaphore_signal(barrier, inc=1, device_id=device(me + plane), device_id_type=MESH)

    neighbours = (z + Z - 1) // Z + (2 * Z - 2 - z) // Z
    pl.semaphore_wait(barrier, plane - 1 + neighbours)


def dispatch_kernel(
    plane, grad_ref, normed_ref, hot_ref, rows_ref, held, stage, line_send, line_recv, send, recv
):
    me, z, p = position(plane)
    cap, width = stage.shape[3], stage.shape[4]
    sources = (grad_ref, normed_ref)

    def line_copy(a, way, step, source, origin):
        return pltpu.make_async_remote_copy(
            src_ref=source,
            dst_ref=held.at[a, origin],
            send_sem=line_send.at[a, way, step],
            recv_sem=line_recv.at[a, way, step],
            device_id=device(me + plane if way == 0 else me - plane),
            device_id_type=MESH,
        )

    def plane_copy(a, origin, q, sender, target):
        return pltpu.make_async_remote_copy(
            src_ref=stage.at[a, origin, q],
            dst_ref=rows_ref.at[a, origin * plane + sender],
            send_sem=send.at[a, origin, q],
            recv_sem=recv.at[a, origin, sender],
            device_id=device(z * plane + target),
            device_id_type=MESH,
        )

    def spread(a, origin, block):
        hot = hot_ref[origin].reshape(plane * cap, -1)

        def chunk(c, carry):
            columns = pl.ds(pl.multiple_of(c * COLUMNS, COLUMNS), COLUMNS)
            picked = jnp.dot(hot, block[:, columns], preferred_element_type=jnp.float32)
            stage[a, origin, :, :, columns] = picked.astype(jnp.bfloat16).reshape(
                plane, cap, COLUMNS
            )
            return carry

        lax.fori_loop(0, width // COLUMNS, chunk, 0)

        def post(d, carry):
            q = (p + d) % plane
            plane_copy(a, origin, q, p, q).start()
            return carry

        lax.fori_loop(1, plane, post, 0)
        rows_ref[a, origin * plane + p] = stage[a, origin, p]

    greet(plane)
    can_go = (z < Z - 1, z > 0)
    for a in range(2):
        for way in range(2):

            @pl.when(can_go[way])
            def _(a=a, way=way):
                line_copy(a, way, 0, sources[a], z).start()

    for a in range(2):
        spread(a, z, sources[a])
    for step in range(1, Z):
        for a in range(2):
            for way in range(2):
                origin = z - step if way == 0 else z + step
                there = z >= step if way == 0 else z + step < Z

                @pl.when(there)
                def _(a=a, way=way, step=step, origin=origin):
                    line_copy(a, way, step - 1, held.at[a, origin], origin).wait_recv()
                    if step < Z - 1:

                        @pl.when(can_go[way])
                        def _():
                            line_copy(a, way, step, held.at[a, origin], origin).start()

                    spread(a, origin, held.at[a, origin])

    for a in range(2):
        for way in range(2):
            for step in range(Z - 1):
                origin = z - step if way == 0 else z + step
                there = z >= step if way == 0 else z + step < Z

                @pl.when(there & can_go[way])
                def _(a=a, way=way, step=step, origin=origin):
                    line_copy(a, way, step, held.at[a, origin], origin).wait_send()

    def finish(i, carry):
        a, origin, d = i // (Z * plane), (i // plane) % Z, i % plane

        @pl.when(d > 0)
        def _():
            q = (p + d) % plane
            plane_copy(a, origin, q, p, q).wait_send()
            plane_copy(a, origin, q, q, q).wait_recv()

        return carry

    lax.fori_loop(0, 2 * Z * plane, finish, 0)


def combine_kernel(
    plane, out_rows, hot_ref, sum_ref, back, inc, leave, line_send, line_recv, send, recv
):
    me, z, p = position(plane)
    cap, width = back.shape[3], back.shape[4]

    def plane_copy(a, origin, q, sender):
        return pltpu.make_async_remote_copy(
            src_ref=out_rows.at[a, origin * plane + q],
            dst_ref=back.at[a, origin, sender],
            send_sem=send.at[a, origin, q],
            recv_sem=recv.at[a, origin, sender],
            device_id=device(z * plane + q),
            device_id_type=MESH,
        )

    def line_copy(a, way, origin):
        return pltpu.make_async_remote_copy(
            src_ref=leave.at[a, origin],
            dst_ref=inc.at[a, way, origin],
            send_sem=line_send.at[a, origin],
            recv_sem=line_recv.at[a, way, origin],
            device_id=device(me + plane if way == 0 else me - plane),
            device_id_type=MESH,
        )

    def post(a, origin):
        def one(d, carry):
            plane_copy(a, origin, (p + d) % plane, p).start()
            return carry

        lax.fori_loop(1, plane, one, 0)

    def gather(a, origin):
        back[a, origin, p] = out_rows[a, origin * plane + p]

        def one(d, carry):
            q = (p + d) % plane
            plane_copy(a, origin, q, q).wait_recv()
            return carry

        lax.fori_loop(1, plane, one, 0)

    def each_chunk(body):
        def chunk(c, carry):
            body(pl.ds(pl.multiple_of(c * COLUMNS, COLUMNS), COLUMNS))
            return carry

        lax.fori_loop(0, width // COLUMNS, chunk, 0)

    def partial(a, origin, columns):
        rows = back[a, origin, :, :, columns].reshape(plane * cap, COLUMNS)
        return jnp.dot(hot_ref[origin], rows, preferred_element_type=jnp.float32)

    greet(plane)
    comes = (z > 0, z < Z - 1)

    def far(way, step):
        origin = z + step if way == 0 else z - step
        return origin, (z + step < Z if way == 0 else z >= step)

    for step in range(Z - 1, 0, -1):
        for a in range(2):
            for way in range(2):
                origin, there = far(way, step)

                @pl.when(there)
                def _(a=a, origin=origin):
                    post(a, origin)

    for a in range(2):
        post(a, z)

    for step in range(Z - 1, 0, -1):
        for a in range(2):
            for way in range(2):
                origin, there = far(way, step)

                @pl.when(there)
                def _(a=a, way=way, step=step, origin=origin):
                    gather(a, origin)
                    if step == Z - 1:

                        @each_chunk
                        def _(columns):
                            leave[a, origin, :, columns] = partial(a, origin, columns).astype(
                                jnp.bfloat16
                            )
                    else:

                        @pl.when(comes[way])
                        def _():
                            line_copy(a, way, origin).wait_recv()

                            @each_chunk
                            def _(columns):
                                earlier = inc[a, way, origin, :, columns].astype(jnp.float32)
                                leave[a, origin, :, columns] = (
                                    partial(a, origin, columns) + earlier
                                ).astype(jnp.bfloat16)

                        @pl.when(jnp.logical_not(comes[way]))
                        def _():
                            @each_chunk
                            def _(columns):
                                leave[a, origin, :, columns] = partial(a, origin, columns).astype(
                                    jnp.bfloat16
                                )

                    line_copy(a, way, origin).start()

    for a in range(2):
        gather(a, z)

        @each_chunk
        def _(columns, a=a):
            sum_ref[a, :, columns] = partial(a, z, columns)

    for a in range(2):
        for way in range(2):

            @pl.when(comes[way])
            def _(a=a, way=way):
                line_copy(a, way, z).wait_recv()

                @each_chunk
                def _(columns):
                    sum_ref[a, :, columns] += inc[a, way, z, :, columns].astype(jnp.float32)

    for step in range(Z - 1, 0, -1):
        for a in range(2):
            for way in range(2):
                origin, there = far(way, step)

                @pl.when(there)
                def _(a=a, way=way, origin=origin):
                    line_copy(a, way, origin).wait_send()

    def finish(i, carry):
        a, origin, d = i // (Z * plane), (i // plane) % Z, i % plane

        @pl.when(d > 0)
        def _():
            plane_copy(a, origin, (p + d) % plane, p).wait_send()

        return carry

    lax.fori_loop(0, 2 * Z * plane, finish, 0)


VM = pl.BlockSpec(memory_space=pltpu.VMEM)


def dispatch(grad_out, normed, hot, plane, cap):
    tokens, width = normed.shape
    return pl.pallas_call(
        functools.partial(dispatch_kernel, plane),
        out_shape=jax.ShapeDtypeStruct((2, Z * plane, cap, width), jnp.bfloat16),
        in_specs=[VM] * 3,
        out_specs=VM,
        scratch_shapes=[
            pltpu.VMEM((2, Z, tokens, width), jnp.bfloat16),
            pltpu.VMEM((2, Z, plane, cap, width), jnp.bfloat16),
            pltpu.SemaphoreType.DMA((2, 2, Z - 1)),
            pltpu.SemaphoreType.DMA((2, 2, Z - 1)),
            pltpu.SemaphoreType.DMA((2, Z, plane)),
            pltpu.SemaphoreType.DMA((2, Z, plane)),
        ],
        compiler_params=pltpu.CompilerParams(
            collective_id=0, has_side_effects=True, vmem_limit_bytes=48 << 20
        ),
    )(grad_out, normed, hot)


def combine(out_rows, hot, tokens, plane):
    _, _, cap, width = out_rows.shape
    return pl.pallas_call(
        functools.partial(combine_kernel, plane),
        out_shape=jax.ShapeDtypeStruct((2, tokens, width), jnp.float32),
        in_specs=[VM] * 2,
        out_specs=VM,
        scratch_shapes=[
            pltpu.VMEM((2, Z, plane, cap, width), jnp.bfloat16),
            pltpu.VMEM((2, 2, Z, tokens, width), jnp.bfloat16),
            pltpu.VMEM((2, Z, tokens, width), jnp.bfloat16),
            pltpu.SemaphoreType.DMA((2, Z)),
            pltpu.SemaphoreType.DMA((2, 2, Z)),
            pltpu.SemaphoreType.DMA((2, Z, plane)),
            pltpu.SemaphoreType.DMA((2, Z, plane)),
        ],
        compiler_params=pltpu.CompilerParams(
            collective_id=1, has_side_effects=True, vmem_limit_bytes=48 << 20
        ),
    )(out_rows, hot)


def places(named):
    tokens = named.shape[-1]
    order = jnp.arange(tokens, dtype=jnp.int32)
    before = (order[:, None] < order[None, :]).astype(jnp.bfloat16)
    return jnp.dot(
        named.astype(jnp.bfloat16), before, preferred_element_type=jnp.float32
    ).astype(jnp.int32)


def row_sums(values):
    return lax.psum(jnp.sum(values, axis=1), "tensor")


def body(attn_parts, resid, norm_gain, w_gate, w_up, w_down, expert_ids, gate_weights, grad_out):
    experts = lax.axis_size("expert")
    plane = experts // Z
    tokens = expert_ids.shape[0]
    capacity = 5 * tokens * expert_ids.shape[1] // (4 * experts)
    cap = -(-capacity // 16) * 16
    width = resid.shape[1]
    me = lax.axis_index("expert")
    z, p = me // plane, me % plane

    table = lax.all_gather(
        jnp.concatenate([expert_ids.T.astype(jnp.float32), gate_weights.T], axis=0), "expert"
    )
    topk = expert_ids.shape[1]
    ids, gates = table[:, :topk].astype(jnp.int32), table[:, topk:]
    slots = jnp.arange(cap, dtype=jnp.int32)
    line_ids = lax.dynamic_index_in_dim(
        ids.reshape(Z, plane, topk, tokens), p, axis=1, keepdims=False
    )
    plane_experts = z * plane + jnp.arange(plane, dtype=jnp.int32)
    named = jnp.any(line_ids[:, None] == plane_experts[None, :, None, None], axis=2)
    hot = (
        named[:, :, None, :] & (places(named)[:, :, None, :] == slots[None, None, :, None])
    ).astype(jnp.bfloat16)
    hot_back = hot.reshape(Z, plane * cap, tokens).transpose(0, 2, 1)
    here = ids == me
    taken = jnp.any(here, axis=1)
    gate_here = jnp.sum(jnp.where(here, gates, 0.0), axis=1)
    row_gate = jnp.sum(
        jnp.where(
            taken[:, None, :] & (places(taken)[:, None, :] == slots[None, :, None]),
            gate_here[:, None, :],
            0.0,
        ),
        axis=2,
    ).reshape(experts * cap, 1)

    attention = lax.psum_scatter(
        attn_parts[0], "tensor", scatter_dimension=1, tiled=True
    ).astype(jnp.float32)
    hidden_in = resid.astype(jnp.float32) + attention
    inv_rms = lax.rsqrt(row_sums(hidden_in * hidden_in) / D + epsilon)
    normed = (hidden_in * inv_rms[:, None] * norm_gain[None, :]).astype(jnp.bfloat16)

    arrived = dispatch(grad_out, normed, hot, plane, cap).reshape(2, experts * cap, width)
    grad_rows, rows = arrived[0], arrived[1]
    gate_part = jnp.dot(rows, w_gate[0], preferred_element_type=jnp.float32)
    up_part = jnp.dot(rows, w_up[0], preferred_element_type=jnp.float32)
    grad_part = jnp.dot(grad_rows, w_down[0].T, preferred_element_type=jnp.float32)
    summed = lax.psum(
        jnp.stack([gate_part, up_part, grad_part]).astype(jnp.bfloat16), "tensor"
    ).astype(jnp.float32)
    gate_pre, up_pre, grad_act = summed[0], summed[1], summed[2] * row_gate
    sigmoid_gate = jax.nn.sigmoid(gate_pre)
    swish = gate_pre * sigmoid_gate
    activation = (swish * up_pre).astype(jnp.bfloat16)
    expert_out = (
        jnp.dot(activation, w_down[0], preferred_element_type=jnp.float32) * row_gate
    ).astype(jnp.bfloat16)
    grad_gate = grad_act * up_pre * sigmoid_gate * (1.0 + gate_pre * (1.0 - sigmoid_gate))
    grad_up = grad_act * swish
    grad_expert = (
        jnp.dot(grad_gate.astype(jnp.bfloat16), w_gate[0].T, preferred_element_type=jnp.float32)
        + jnp.dot(grad_up.astype(jnp.bfloat16), w_up[0].T, preferred_element_type=jnp.float32)
    ).astype(jnp.bfloat16)
    out_rows = jnp.stack([expert_out, grad_expert]).reshape(2, experts, cap, width)
    sums = combine(out_rows, hot_back, tokens, plane)
    moe, grad_normed = sums[0], sums[1]

    output = (hidden_in + moe).astype(jnp.bfloat16)
    scaled = grad_normed * norm_gain[None, :]
    inner = row_sums(hidden_in * scaled)
    grad_input = (
        grad_out.astype(jnp.float32)
        + inv_rms[:, None] * scaled
        - hidden_in * (inv_rms**3 * inner / D)[:, None]
    )
    return (output, grad_input.astype(jnp.bfloat16))


def solution(mesh):
    return jax.shard_map(
        body,
        mesh=mesh,
        in_specs=(
            P("tensor", "expert", None),
            P("expert", "tensor"),
            P("tensor"),
            P("expert", "tensor", None),
            P("expert", "tensor", None),
            P("expert", None, "tensor"),
            P("expert", None),
            P("expert", None),
            P("expert", "tensor"),
        ),
        out_specs=(P("expert", "tensor"), P("expert", "tensor")),
        check_vma=False,
    )
```

time: 337 us -> 300 us (0.89)
  waiting for transfers between devices: 224 us -> 35.6 us
  Pallas kernels: 0 us -> 165 us
  blocking collectives: 7.18 us -> 37 us
  starting transfers between devices: 23.7 us -> 0.08 us
  matrix products: 42.1 us -> 21.8 us
  other arithmetic: 10.2 us -> 17.6 us
  local copies, waits for them, and re-layouts: 14.3 us -> 7.65 us
    all_to_all x4 -> x0, waiting for transfers between devices: 185 us -> none  [the longest x2 95 us: to_source(): lax.all_to_all(blocks, 'expert', split_axis=0, concat_axis=0, tiled=True)]
    pallas_call x0 -> x2, Pallas kernels: none -> 165 us  [the longest x1 86.8 us: combine(): pl.pallas_call(functools.partial(combine_kernel, plane), out_shape=jax.Sh...]
    all_gather x0 -> x1, blocking collectives: none -> 23.8 us  [body(): lax.all_gather(jnp.concatenate([expert_ids.T.astype(jnp.float32), gate_we...]
    all_to_all x4 -> x0, starting transfers between devices: 23.6 us -> none  [the longest x2 11.9 us: to_source(): lax.all_to_all(blocks, 'expert', split_axis=0, concat_axis=0, tiled=True)]
    reduce_scatter x1, waiting for transfers between devices: 13.1 us -> 0.02 us  [body(): lax.psum_scatter(attn_parts[0], 'tensor', scatter_dimension=1, tiled=True)]
    dot_general x7 -> x5, matrix products: 25.8 us -> 13.6 us  [the longest x1 5.49 us: body(): jnp.dot(grad_up.astype(jnp.bfloat16), w_up[0].T, preferred_element_type=j...]
    gather x2 -> x0, local copies, waits for them, and re-layouts: 11.5 us -> none  [body(): jnp.take(returned, slot_index.reshape(-1), axis=0)]
    psum x1, waiting for transfers between devices: 25 us -> 34.9 us  [body(): lax.psum(jnp.stack([gate_part, up_part, grad_part]).astype(jnp.bfloat16),...]
  transfers between devices with their start and end apart: 6 -> 2, of which waited for: 6 -> 1; matrix products, arithmetic and copies ran while one was open for 9% -> 2% of each run, Pallas kernels for 0% -> 0%
where the time goes in v1:
time: 300 us; the launch traced here: 299 us
  Pallas kernels  165 us (55%)
  blocking collectives  37 us (12%)
  waiting for transfers between devices  35.6 us (12%)
  matrix products  21.8 us (7%)
  other arithmetic  17.6 us (6%)
  between operations  14.3 us (5%)
  local copies, waits for them, and re-layouts  7.65 us (3%)
    pallas_call x1, Pallas kernels, combine(): pl.pallas_call(functools.partial(combine_kernel, plane), out_shape=jax.Sh...  86.8 us
    pallas_call x1, Pallas kernels, dispatch(): pl.pallas_call(functools.partial(dispatch_kernel, plane), out_shape=jax.S...  78.5 us
    psum x1, waiting for transfers between devices, body(): lax.psum(jnp.stack([gate_part, up_part, grad_part]).astype(jnp.bfloat16),...  34.9 us
    all_gather x1, blocking collectives, body(): lax.all_gather(jnp.concatenate([expert_ids.T.astype(jnp.float32), gate_we...  23.8 us
    psum x2, blocking collectives, row_sums(): return lax.psum(jnp.sum(values, axis=1), 'tensor')  13.2 us
  transfers between devices with their start and end apart: 2, of which 1 were waited for; matrix products, arithmetic and copies ran while one was open for 2% of the time, Pallas kernels for 0%

profile of v1, /device:TPU:17, one launch (start us, length us, event | category | flops | bytes accessed | tf_op | source)
XLA Modules:
  0.0 299.4 jit_solution(4583022886182003946)
XLA Ops:
  7.2 0.0 copy-start
  7.2 0.0 reduce-scatter.2.cloned.1.call-start
  7.2 0.7 reduce-scatter.2.cloned.1.call-update
  7.9 0.0 all-reduce.2.cloned.1.call-start
  8.0 0.8 convert_bitcast_fusion
  8.8 0.7 pad_maximum_fusion.2
  9.5 23.8 %all-gather = f32[128,128]{1,0:T(8,128)S(1)} all-gather(f32[8,128]{1,0:T(8,128)S(1)} %pad_maximum_fusion.2), channel_id=2, replica_groups=mesh['expert'=16,'tensor'=2] {'expert'}, dimensions={0}, use_global_device_ids=true | all-gather | bytes 69632 | tf_op jit(solution)/shard_map/all_gather | solution.py:370
  33.4 0.1 compare_reduce_fusion
  33.5 0.1 convolution_convert_fusion.1
  33.6 0.1 fusion.38.hot_ref
  33.7 0.0 reduce-scatter.2.cloned.1.call-done
  33.8 1.5 multiply_reduce_fusion.1
  35.2 9.9 %psum.21 = f32[128]{0:T(128)S(1)} all-reduce(f32[128]{0:T(128)S(1)} %multiply_reduce_fusion.1), channel_id=1, replica_groups=mesh['expert'=16,'tensor'=2] {'tensor'}, use_global_device_ids=true, to_apply=%region_2.3 | all-reduce | flops 128 | bytes 1024 | tf_op jit(solution)/shard_map/psum | solution.py:357
  45.1 0.0 copy-start.12
  45.1 0.0 copy-start.6
  45.1 1.4 multiply_convert_fusion.5.normed_ref
  46.6 0.0 copy-start.2
  46.6 1.0 copy-done.2
  47.6 78.5 %shard_map.104 = bf16[2,16,48,2048]{3,2,1,0:T(8,128)(2,1)} custom-call(bf16[128,2048]{1,0:T(8,128)(2,1)S(1)} %copy-done.2, bf16[128,2048]{1,0:T(8,128)(2,1)S(1)} %multiply_convert_fusion.5.normed_ref, bf16[4,4,48,128]{3,2,1,0:T(8,128)(2,1)S(1)} %fusion.38.hot_ref), custom_call_target="tpu_custom_call" | custom-call | tf_op jit(solution)/shard_map/pallas_call | solution.py:306
  126.1 0.0 copy-done.12
  126.1 0.0 copy-done.6
  126.1 0.0 copy-start.10
  126.2 3.6 %fusion.52 = (bf16[1,16,48,2048]{3,2,1,0:T(8,128)(2,1)S(1)}, bf16[1,16,48,2048]{3,2,1,0:T(8,128)(2,1)S(1)}) fusion(bf16[2,16,48,2048]{3,2,1,0:T(8,128)(2,1)} %shard_map.104), kind=kLoop, calls=%fused_computation.68 | loop fusion | bytes 12582912 | tf_op jit(solution)/shard_map/slice | solution.py:405
  129.7 0.2 copy-done.10
  129.9 2.6 fusion.23
  132.5 0.0 copy-done
  132.5 0.0 copy-start.8
  132.5 2.6 fusion.26
  135.1 0.0 copy-done.8
  135.1 2.6 fusion.20
  137.8 2.0 pad_maximum_fusion.1
  139.8 0.0 all-reduce.2.cloned.1.call-update
  139.8 0.1 convolution_convert_fusion
  140.0 0.2 select_reduce_fusion
  140.2 0.1 mul.105
  140.3 1.0 copy.17
  141.3 0.3 copy.19
  141.6 0.1 eq.74
  141.6 1.1 fusion.42.hot_ref
  142.8 34.9 %all-reduce.2.cloned.1.call-done = bf16[3,768,768]{2,1,0:T(8,128)(2,1)} async-done(((bf16[3,768,768]{2,1,0:T(8,128)(2,1)}), bf16[3,768,768]{2,1,0:T(8,128)(2,1)}) %all-reduce.2.cloned.1.call-update) | async-done | bytes 3538960 | tf_op jit(solution)/shard_map/psum | solution.py:409
  177.7 2.6 convert_element_type.76
  180.3 0.0 copy-start.9
  180.3 5.2 %fusion.6 = f32[768,2048]{1,0:T(8,128)} fusion(bf16[1,2048,768]{2,1,0:T(8,128)(2,1)S(1)} %copy-done, f32[3,768,768]{2,1,0:T(8,128)S(1)} %convert_element_type.76, f32[768]{0:T(1024)S(1)} %mul.105), kind=kOutput, calls=%fused_computation.10 | convolution fusion | flops 2422407168 | bytes 16518144 | tf_op jit(solution)/shard_map/dot_general | solution.py:422
  185.5 0.0 copy-done.9
  185.5 0.0 copy-start.11
  185.5 3.0 %multiply_convert_fusion = bf16[768,2048]{1,0:T(8,128)(2,1)S(1)} fusion(bf16[1,768,2048]{2,1,0:T(8,128)(2,1)S(1)} %copy-done.9, f32[768]{0:T(1024)S(1)} %mul.105, f32[3,768,768]{2,1,0:T(8,128)S(1)} %convert_element_type.76), kind=kOutput, calls=%fused_computation.2 | convolution fusion | flops 2422603776 | bytes 11014144 | tf_op jit(solution)/shard_map/dot_general | solution.py:417
  188.5 0.0 copy-done.11
  188.5 5.5 %add_convert_fusion = bf16[768,2048]{1,0:T(8,128)(2,1)S(1)} fusion(f32[768,2048]{1,0:T(8,128)} %fusion.6, bf16[1,2048,768]{2,1,0:T(8,128)(2,1)S(1)} %copy-done.11, f32[3,768,768]{2,1,0:T(8,128)S(1)} %convert_element_type.76, f32[768]{0:T(1024)S(1)} %mul.105), kind=kOutput, calls=%fused_computation.1 | convolution fusion | flops 2423193600 | bytes 17305600 | tf_op jit(solution)/shard_map/dot_general | solution.py:423
  194.0 3.2 %pad_maximum_fusion.out_rows = bf16[2,16,48,2048]{3,2,1,0:T(8,128)(2,1)} fusion(bf16[1,16,48,2048]{3,2,1,0:T(8,128)(2,1)S(1)} %bitcast.80, bf16[1,16,48,2048]{3,2,1,0:T(8,128)(2,1)S(1)} %bitcast.79), kind=kLoop, calls=%fused_computation | loop fusion | flops 3145728 | bytes 12582912 | tf_op jit(solution)/shard_map/stack | solution.py:425
  197.2 0.0 copy-start.3
  197.2 0.0 copy-start.4
  197.2 0.0 copy-start.13
  197.2 0.0 copy-start.7
  197.2 86.8 %shard_map.105 = f32[2,128,2048]{2,1,0:T(8,128)S(1)} custom-call(bf16[2,16,48,2048]{3,2,1,0:T(8,128)(2,1)} %pad_maximum_fusion.out_rows, bf16[4,128,192]{2,1,0:T(8,128)(2,1)S(1)} %fusion.42.hot_ref), custom_call_target="tpu_custom_call" | custom-call | tf_op jit(solution)/shard_map/pallas_call | solution.py:327
  284.0 0.0 copy-start.1
  284.0 1.3 copy-done.1
  285.3 0.0 copy-done.3
  285.3 0.0 copy-done.4
  285.3 0.0 copy-done.5
  285.4 0.3 multiply_reduce_fusion
  285.7 3.3 %psum.23 = f32[128]{0:T(128)S(1)} all-reduce(f32[128]{0:T(128)S(1)} %multiply_reduce_fusion), channel_id=1, replica_groups=mesh['expert'=16,'tensor'=2] {'tensor'}, use_global_device_ids=true, to_apply=%region_9.10 | all-reduce | flops 128 | bytes 1024 | tf_op jit(solution)/shard_map/psum | solution.py:357
  289.0 0.0 copy-done.13
  289.0 0.0 copy-done.7
  289.0 3.5 %subtract_convert_fusion = (bf16[128,2048]{1,0:T(8,128)(2,1)}, bf16[128,2048]{1,0:T(8,128)(2,1)}) fusion(bf16[128,2048]{1,0:T(8,128)(2,1)} %grad_ref.1, f32[2,128,2048]{2,1,0:T(8,128)} %copy-done.1, bf16[128,2048]{1,0:T(8,128)(2,1)} %reduce-scatter.2.cloned.1.call-done, bf16[128,2048]{1,0:T(8,128)(2,1)} %param.10, f32[128]{0:T(128)S(1)} %fusion.47, ...), kind=kLoop, calls=%fused_computation.36 | loop fusion | flops 3145728 | bytes 4727808 | tf_op jit(solution)/shard_map/convert_element_type | solution.py:437
  (10 shorter events, 0.2 us)
Async XLA Ops:
  7.2 125.3 %copy-start = (bf16[1,2048,768]{2,1,0:T(8,128)(2,1)S(1)}, bf16[1,2048,768]{2,1,0:T(8,128)(2,1)}, u32[]{:S(2)}) copy-start(bf16[1,2048,768]{2,1,0:T(8,128)(2,1)} %param.12) | copy-start | bytes 9437188
  7.2 26.6 %reduce-scatter.2.cloned.1.call-start = ((), (), s32[]{:S(2)}) async-start(), calls=%async_computation.1 | async-start | bytes 1572864 | tf_op jit(solution)/shard_map/reduce_scatter | solution.py:397
  7.9 169.8 %all-reduce.2.cloned.1.call-start = ((), (), s32[]{:S(2)}) async-start(), calls=%async_computation.2 | async-start | bytes 7077888 | tf_op jit(solution)/shard_map/psum | solution.py:409
  45.1 81.0 %copy-start.12 = (f32[128]{0:T(128)}, f32[128]{0:T(128)S(1)}, u32[]{:S(2)}) copy-start(f32[128]{0:T(128)S(1)} %psum.21) | copy-start | bytes 1540
  45.1 81.0 %copy-start.6 = (f32[128]{0:T(128)}, f32[128]{0:T(128)S(1)}, u32[]{:S(2)}) copy-start(f32[128]{0:T(128)S(1)} %add_rsqrt_fusion) | copy-start | bytes 1540
  46.6 1.0 copy-start.2
  126.1 3.7 %copy-start.10 = (bf16[1,2048,768]{2,1,0:T(8,128)(2,1)S(1)}, bf16[1,2048,768]{2,1,0:T(8,128)(2,1)}, u32[]{:S(2)}) copy-start(bf16[1,2048,768]{2,1,0:T(8,128)(2,1)} %param.13) | copy-start | bytes 9437188
  132.5 2.6 copy-start.8
  180.3 5.2 %copy-start.9 = (bf16[1,768,2048]{2,1,0:T(8,128)(2,1)S(1)}, bf16[1,768,2048]{2,1,0:T(8,128)(2,1)}, u32[]{:S(2)}) copy-start(bf16[1,768,2048]{2,1,0:T(8,128)(2,1)} %param.14) | copy-start | bytes 9437188
  185.5 3.0 %copy-start.11 = (bf16[1,2048,768]{2,1,0:T(8,128)(2,1)S(1)}, bf16[1,2048,768]{2,1,0:T(8,128)(2,1)}, u32[]{:S(2)}) copy-start(bf16[1,2048,768]{2,1,0:T(8,128)(2,1)} %param.13) | copy-start | bytes 9437188
  197.2 88.1 %copy-start.3 = (bf16[128,2048]{1,0:T(8,128)(2,1)S(1)}, bf16[128,2048]{1,0:T(8,128)(2,1)}, u32[]{:S(2)}) copy-start(bf16[128,2048]{1,0:T(8,128)(2,1)} %param.10) | copy-start | bytes 1572868
  197.2 88.1 %copy-start.4 = (bf16[128,2048]{1,0:T(8,128)(2,1)S(1)}, bf16[128,2048]{1,0:T(8,128)(2,1)}, u32[]{:S(2)}) copy-start(bf16[128,2048]{1,0:T(8,128)(2,1)} %reduce-scatter.2.cloned.1.call-done) | copy-start | bytes 1572868
  197.2 88.1 %copy-start.5 = (f32[2048]{0:T(1024)S(1)}, f32[2048]{0:T(1024)}, u32[]{:S(2)}) copy-start(f32[2048]{0:T(1024)} %param.11) | copy-start | bytes 24580
  197.2 91.8 %copy-start.13 = (f32[128]{0:T(128)S(1)}, f32[128]{0:T(128)}, u32[]{:S(2)}) copy-start(f32[128]{0:T(128)} %copy-done.12) | copy-start | bytes 1540
  197.2 91.8 %copy-start.7 = (f32[128]{0:T(128)S(1)}, f32[128]{0:T(128)}, u32[]{:S(2)}) copy-start(f32[128]{0:T(128)} %copy-done.6) | copy-start | bytes 1540
  284.0 1.4 copy-start.1
Sparse Core Ops, SparseCore 0:
  10.3 10.3 reduce-scatter.1
  139.9 37.7 all-reduce.1

commit v2 on v1

--- a/solution.py
+++ b/solution.py
@@ -24,9 +24,15 @@
     return me, me // plane, me % plane
 
 
-def greet(plane):
+def partner():
+    return (lax.axis_index("expert"), 1 - lax.axis_index("tensor"))
+
+
+def greet(plane, pair):
     me, z, p = position(plane)
     barrier = pltpu.get_barrier_semaphore()
+    if pair:
+        pl.semaphore_signal(barrier, inc=1, device_id=partner(), device_id_type=MESH)
 
     def hello(d, carry):
         pl.semaphore_signal(
@@ -45,15 +51,129 @@
         pl.semaphore_signal(barrier, inc=1, device_id=device(me + plane), device_id_type=MESH)
 
     neighbours = (z + Z - 1) // Z + (2 * Z - 2 - z) // Z
-    pl.semaphore_wait(barrier, plane - 1 + neighbours)
+    pl.semaphore_wait(barrier, plane - 1 + int(pair) + neighbours)
 
 
 def dispatch_kernel(
-    plane, grad_ref, normed_ref, hot_ref, rows_ref, held, stage, line_send, line_recv, send, recv
+    plane,
+    attn_ref,
+    resid_ref,
+    gain_ref,
+    grad_ref,
+    table_ref,
+    rows_ref,
+    hidden_ref,
+    inv_ref,
+    hot_ref,
+    gate_ref,
+    held,
+    stage,
+    normed,
+    other,
+    stat,
+    tables,
+    line_send,
+    line_recv,
+    send,
+    recv,
+    table_send,
+    table_recv,
+    pair_send,
+    pair_recv,
 ):
     me, z, p = position(plane)
     cap, width = stage.shape[3], stage.shape[4]
-    sources = (grad_ref, normed_ref)
+    tokens = table_ref.shape[1]
+    topk = table_ref.shape[0] // 2
+    side = lax.axis_index("tensor")
+    sources = (grad_ref, normed)
+
+    def pair_copy(i, source, target):
+        return pltpu.make_async_remote_copy(
+            src_ref=source,
+            dst_ref=target,
+            send_sem=pair_send.at[i],
+            recv_sem=pair_recv.at[i],
+            device_id=partner(),
+            device_id_type=MESH,
+        )
+
+    def half(of):
+        return pl.ds(pl.multiple_of(of * width, width), width)
+
+    attn_copy = pair_copy(0, attn_ref.at[:, half(1 - side)], other)
+    stat_copy = pair_copy(1, stat.at[0], stat.at[1])
+
+    def table_copy(way, step, source, origin):
+        return pltpu.make_async_remote_copy(
+            src_ref=source,
+            dst_ref=tables.at[origin],
+            send_sem=table_send.at[way, step],
+            recv_sem=table_recv.at[way, step],
+            device_id=device(me + plane if way == 0 else me - plane),
+            device_id_type=MESH,
+        )
+
+    def find_slots(origin, table):
+        count = max(16, plane)
+        expert = (z * plane + lax.broadcasted_iota(jnp.int32, (count, tokens), 0)).astype(
+            jnp.float32
+        )
+        named = jnp.zeros((count, tokens), jnp.float32)
+        gates = jnp.zeros((count, tokens), jnp.float32)
+        for k in range(topk):
+            hit = table[k : k + 1, :] == expert
+            named = jnp.where(hit, 1.0, named)
+            gates = jnp.where(hit, table[topk + k : topk + k + 1, :], gates)
+        before = jnp.where(
+            lax.broadcasted_iota(jnp.int32, (tokens, tokens), 0)
+            < lax.broadcasted_iota(jnp.int32, (tokens, tokens), 1),
+            1.0,
+            0.0,
+        ).astype(jnp.bfloat16)
+        earlier = jnp.dot(named.astype(jnp.bfloat16), before, preferred_element_type=jnp.float32)
+        slot = jnp.where(named > 0.5, earlier, -1.0)
+        number = lax.broadcasted_iota(jnp.int32, (cap, tokens), 0).astype(jnp.float32)
+        for e in range(plane):
+            own = slot[e : e + 1, :] == number
+            hot_ref[origin, e * cap : (e + 1) * cap, :] = jnp.where(own, 1.0, 0.0).astype(
+                jnp.bfloat16
+            )
+            weight = jnp.sum(jnp.where(own, gates[e : e + 1, :], 0.0), axis=1, keepdims=True)
+            gate_ref[origin, e * cap : (e + 1) * cap, :] = jnp.broadcast_to(weight, (cap, tokens))
+
+    def each_chunk(body):
+        def chunk(c, carry):
+            body(pl.ds(pl.multiple_of(c * COLUMNS, COLUMNS), COLUMNS))
+            return carry
+
+        lax.fori_loop(0, width // COLUMNS, chunk, 0)
+
+    def norm():
+        stat[0] = jnp.zeros((tokens, 128), jnp.float32)
+        attn_copy.wait_recv()
+
+        def chunk(c, carry):
+            columns = pl.ds(pl.multiple_of(c * COLUMNS, COLUMNS), COLUMNS)
+            own = pl.ds(pl.multiple_of(side * width + c * COLUMNS, COLUMNS), COLUMNS)
+            value = resid_ref[:, columns].astype(jnp.float32) + (
+                attn_ref[:, own].astype(jnp.float32) + other[:, columns].astype(jnp.float32)
+            )
+            hidden_ref[:, columns] = value
+            squares = jnp.sum(value * value, axis=1, keepdims=True)
+            stat[0] += jnp.broadcast_to(squares, (tokens, 128))
+            return carry
+
+        lax.fori_loop(0, width // COLUMNS, chunk, 0)
+        stat_copy.start()
+        stat_copy.wait_recv()
+        inv_ref[...] = lax.rsqrt((stat[0] + stat[1]) / D + epsilon)
+
+        @each_chunk
+        def _(columns):
+            normed[:, columns] = (
+                hidden_ref[:, columns] * inv_ref[:, 0:1] * gain_ref[:, columns]
+            ).astype(jnp.bfloat16)
 
     def line_copy(a, way, step, source, origin):
         return pltpu.make_async_remote_copy(
@@ -76,17 +196,16 @@
         )
 
     def spread(a, origin, block):
-        hot = hot_ref[origin].reshape(plane * cap, -1)
-
-        def chunk(c, carry):
-            columns = pl.ds(pl.multiple_of(c * COLUMNS, COLUMNS), COLUMNS)
-            picked = jnp.dot(hot, block[:, columns], preferred_element_type=jnp.float32)
+        @each_chunk
+        def _(columns):
+            picked = jnp.dot(
+                hot_ref[origin], block[:, columns], preferred_element_type=jnp.float32
+            )
+            if a == 0:
+                picked = picked * gate_ref[origin, :, 0:1]
             stage[a, origin, :, :, columns] = picked.astype(jnp.bfloat16).reshape(
                 plane, cap, COLUMNS
             )
-            return carry
-
-        lax.fori_loop(0, width // COLUMNS, chunk, 0)
 
         def post(d, carry):
             q = (p + d) % plane
@@ -96,17 +215,25 @@
         lax.fori_loop(1, plane, post, 0)
         rows_ref[a, origin * plane + p] = stage[a, origin, p]
 
-    greet(plane)
+    greet(plane, True)
     can_go = (z < Z - 1, z > 0)
-    for a in range(2):
+    attn_copy.start()
+
+    def set_out(a):
         for way in range(2):
 
             @pl.when(can_go[way])
-            def _(a=a, way=way):
+            def _(way=way):
+                if a == 0:
+                    table_copy(way, 0, table_ref, z).start()
                 line_copy(a, way, 0, sources[a], z).start()
 
-    for a in range(2):
-        spread(a, z, sources[a])
+    set_out(0)
+    find_slots(z, table_ref[...])
+    spread(0, z, grad_ref)
+    norm()
+    set_out(1)
+    spread(1, z, normed)
     for step in range(1, Z):
         for a in range(2):
             for way in range(2):
@@ -115,6 +242,14 @@
 
                 @pl.when(there)
                 def _(a=a, way=way, step=step, origin=origin):
+                    if a == 0:
+                        table_copy(way, step - 1, tables.at[origin], origin).wait_recv()
+                        if step < Z - 1:
+
+                            @pl.when(can_go[way])
+                            def _():
+                                table_copy(way, step, tables.at[origin], origin).start()
+
                     line_copy(a, way, step - 1, held.at[a, origin], origin).wait_recv()
                     if step < Z - 1:
 
@@ -122,6 +257,8 @@
                         def _():
                             line_copy(a, way, step, held.at[a, origin], origin).start()
 
+                    if a == 0:
+                        find_slots(origin, tables[origin])
                     spread(a, origin, held.at[a, origin])
 
     for a in range(2):
@@ -132,7 +269,12 @@
 
                 @pl.when(there & can_go[way])
                 def _(a=a, way=way, step=step, origin=origin):
+                    if a == 0:
+                        table_copy(way, step, tables.at[origin], origin).wait_send()
                     line_copy(a, way, step, held.at[a, origin], origin).wait_send()
+
+    attn_copy.wait_send()
+    stat_copy.wait_send()
 
     def finish(i, carry):
         a, origin, d = i // (Z * plane), (i // plane) % Z, i % plane
@@ -149,7 +291,7 @@
 
 
 def combine_kernel(
-    plane, out_rows, hot_ref, sum_ref, back, inc, leave, line_send, line_recv, send, recv
+    plane, out_rows, hot_ref, gate_ref, sum_ref, back, inc, leave, line_send, line_recv, send, recv
 ):
     me, z, p = position(plane)
     cap, width = back.shape[3], back.shape[4]
@@ -200,9 +342,18 @@
 
     def partial(a, origin, columns):
         rows = back[a, origin, :, :, columns].reshape(plane * cap, COLUMNS)
-        return jnp.dot(hot_ref[origin], rows, preferred_element_type=jnp.float32)
-
-    greet(plane)
+        first = (((0,), (0,)), ((), ()))
+        hot = hot_ref[origin]
+        if a == 1:
+            return lax.dot_general(hot, rows, first, preferred_element_type=jnp.float32)
+        weight = hot.astype(jnp.float32) * gate_ref[origin]
+        high = weight.astype(jnp.bfloat16)
+        low = (weight - high.astype(jnp.float32)).astype(jnp.bfloat16)
+        return lax.dot_general(
+            high, rows, first, preferred_element_type=jnp.float32
+        ) + lax.dot_general(low, rows, first, preferred_element_type=jnp.float32)
+
+    greet(plane, False)
     comes = (z > 0, z < Z - 1)
 
     def far(way, step):
@@ -301,33 +452,140 @@
 VM = pl.BlockSpec(memory_space=pltpu.VMEM)
 
 
-def dispatch(grad_out, normed, hot, plane, cap):
-    tokens, width = normed.shape
+def expert_kernel(
+    rows_ref, gate_ref, up_ref, down_ref, out_ref, mine, theirs, send, recv
+):
+    count, part = mine.shape[0], mine.shape[2]
+    width = rows_ref.shape[2]
+    last = (((1,), (1,)), ((), ()))
+    barrier = pltpu.get_barrier_semaphore()
+    pl.semaphore_signal(barrier, inc=1, device_id=partner(), device_id_type=MESH)
+    pl.semaphore_wait(barrier, 1)
+
+    def copy(c):
+        return pltpu.make_async_remote_copy(
+            src_ref=mine.at[c],
+            dst_ref=theirs.at[c],
+            send_sem=send.at[c],
+            recv_sem=recv.at[c],
+            device_id=partner(),
+            device_id_type=MESH,
+        )
+
+    def first_half(c, carry):
+        at = pl.ds(pl.multiple_of(c * part, part), part)
+        rows = rows_ref[1, at, :]
+        mine[c, 0] = jnp.dot(rows, gate_ref[...], preferred_element_type=jnp.float32).astype(
+            jnp.bfloat16
+        )
+        mine[c, 1] = jnp.dot(rows, up_ref[...], preferred_element_type=jnp.float32).astype(
+            jnp.bfloat16
+        )
+        mine[c, 2] = lax.dot_general(
+            rows_ref[0, at, :], down_ref[...], last, preferred_element_type=jnp.float32
+        ).astype(jnp.bfloat16)
+        copy(c).start()
+        return carry
+
+    def second_half(c, carry):
+        at = pl.ds(pl.multiple_of(c * part, part), part)
+        copy(c).wait()
+        gate_pre, up_pre, grad_act = (
+            mine[c, i].astype(jnp.float32) + theirs[c, i].astype(jnp.float32) for i in range(3)
+        )
+        sigmoid_gate = 1.0 / (1.0 + jnp.exp(-gate_pre))
+        swish = gate_pre * sigmoid_gate
+        mine[c, 0] = (swish * up_pre).astype(jnp.bfloat16)
+        mine[c, 1] = (
+            grad_act * up_pre * sigmoid_gate * (1.0 + gate_pre * (1.0 - sigmoid_gate))
+        ).astype(jnp.bfloat16)
+        mine[c, 2] = (grad_act * swish).astype(jnp.bfloat16)
+
+        def chunk(i, inner):
+            columns = pl.ds(pl.multiple_of(i * COLUMNS, COLUMNS), COLUMNS)
+            out_ref[0, at, columns] = jnp.dot(
+                mine[c, 0], down_ref[:, columns], preferred_element_type=jnp.float32
+            ).astype(jnp.bfloat16)
+            out_ref[1, at, columns] = (
+                lax.dot_general(
+                    mine[c, 1], gate_ref[columns, :], last, preferred_element_type=jnp.float32
+                )
+                + lax.dot_general(
+                    mine[c, 2], up_ref[columns, :], last, preferred_element_type=jnp.float32
+                )
+            ).astype(jnp.bfloat16)
+            return inner
+
+        lax.fori_loop(0, width // COLUMNS, chunk, 0)
+        return carry
+
+    lax.fori_loop(0, count, first_half, 0)
+    lax.fori_loop(0, count, second_half, 0)
+
+
+def expert_layer(rows, w_gate, w_up, w_down):
+    _, total, width = rows.shape
+    hidden = w_gate.shape[1]
+    part = 256
+    count = total // part
+    return pl.pallas_call(
+        expert_kernel,
+        out_shape=jax.ShapeDtypeStruct((2, total, width), jnp.bfloat16),
+        in_specs=[VM] * 4,
+        out_specs=VM,
+        scratch_shapes=[
+            pltpu.VMEM((count, 3, part, hidden), jnp.bfloat16),
+            pltpu.VMEM((count, 3, part, hidden), jnp.bfloat16),
+            pltpu.SemaphoreType.DMA((count,)),
+            pltpu.SemaphoreType.DMA((count,)),
+        ],
+        compiler_params=pltpu.CompilerParams(
+            collective_id=2, has_side_effects=True, vmem_limit_bytes=52 << 20
+        ),
+    )(rows, w_gate, w_up, w_down)
+
+
+def dispatch(attn, resid, gain, grad_out, table, plane, cap):
+    tokens, width = resid.shape
     return pl.pallas_call(
         functools.partial(dispatch_kernel, plane),
-        out_shape=jax.ShapeDtypeStruct((2, Z * plane, cap, width), jnp.bfloat16),
-        in_specs=[VM] * 3,
-        out_specs=VM,
+        out_shape=(
+            jax.ShapeDtypeStruct((2, Z * plane, cap, width), jnp.bfloat16),
+            jax.ShapeDtypeStruct((tokens, width), jnp.float32),
+            jax.ShapeDtypeStruct((tokens, 128), jnp.float32),
+            jax.ShapeDtypeStruct((Z, plane * cap, tokens), jnp.bfloat16),
+            jax.ShapeDtypeStruct((Z, plane * cap, tokens), jnp.float32),
+        ),
+        in_specs=[VM] * 5,
+        out_specs=(VM,) * 5,
         scratch_shapes=[
             pltpu.VMEM((2, Z, tokens, width), jnp.bfloat16),
             pltpu.VMEM((2, Z, plane, cap, width), jnp.bfloat16),
+            pltpu.VMEM((tokens, width), jnp.bfloat16),
+            pltpu.VMEM((tokens, width), jnp.bfloat16),
+            pltpu.VMEM((2, tokens, 128), jnp.float32),
+            pltpu.VMEM((Z,) + table.shape, jnp.float32),
             pltpu.SemaphoreType.DMA((2, 2, Z - 1)),
             pltpu.SemaphoreType.DMA((2, 2, Z - 1)),
             pltpu.SemaphoreType.DMA((2, Z, plane)),
             pltpu.SemaphoreType.DMA((2, Z, plane)),
+            pltpu.SemaphoreType.DMA((2, Z - 1)),
+            pltpu.SemaphoreType.DMA((2, Z - 1)),
+            pltpu.SemaphoreType.DMA((2,)),
+            pltpu.SemaphoreType.DMA((2,)),
         ],
         compiler_params=pltpu.CompilerParams(
             collective_id=0, has_side_effects=True, vmem_limit_bytes=48 << 20
         ),
-    )(grad_out, normed, hot)
-
-
-def combine(out_rows, hot, tokens, plane):
+    )(attn, resid, gain, grad_out, table)
+
+
+def combine(out_rows, hot, gate, tokens, plane):
     _, _, cap, width = out_rows.shape
     return pl.pallas_call(
         functools.partial(combine_kernel, plane),
         out_shape=jax.ShapeDtypeStruct((2, tokens, width), jnp.float32),
-        in_specs=[VM] * 2,
+        in_specs=[VM] * 3,
         out_specs=VM,
         scratch_shapes=[
             pltpu.VMEM((2, Z, plane, cap, width), jnp.bfloat16),
@@ -341,16 +599,7 @@
         compiler_params=pltpu.CompilerParams(
             collective_id=1, has_side_effects=True, vmem_limit_bytes=48 << 20
         ),
-    )(out_rows, hot)
-
-
-def places(named):
-    tokens = named.shape[-1]
-    order = jnp.arange(tokens, dtype=jnp.int32)
-    before = (order[:, None] < order[None, :]).astype(jnp.bfloat16)
-    return jnp.dot(
-        named.astype(jnp.bfloat16), before, preferred_element_type=jnp.float32
-    ).astype(jnp.int32)
+    )(out_rows, hot, gate)
 
 
 def row_sums(values):
@@ -364,66 +613,15 @@
     capacity = 5 * tokens * expert_ids.shape[1] // (4 * experts)
     cap = -(-capacity // 16) * 16
     width = resid.shape[1]
-    me = lax.axis_index("expert")
-    z, p = me // plane, me % plane
-
-    table = lax.all_gather(
-        jnp.concatenate([expert_ids.T.astype(jnp.float32), gate_weights.T], axis=0), "expert"
+    table = jnp.concatenate([expert_ids.T.astype(jnp.float32), gate_weights.T], axis=0)
+    rows, hidden_in, inv, hot, gate = dispatch(
+        attn_parts[0], resid, norm_gain[None, :], grad_out, table, plane, cap
     )
-    topk = expert_ids.shape[1]
-    ids, gates = table[:, :topk].astype(jnp.int32), table[:, topk:]
-    slots = jnp.arange(cap, dtype=jnp.int32)
-    line_ids = lax.dynamic_index_in_dim(
-        ids.reshape(Z, plane, topk, tokens), p, axis=1, keepdims=False
-    )
-    plane_experts = z * plane + jnp.arange(plane, dtype=jnp.int32)
-    named = jnp.any(line_ids[:, None] == plane_experts[None, :, None, None], axis=2)
-    hot = (
-        named[:, :, None, :] & (places(named)[:, :, None, :] == slots[None, None, :, None])
-    ).astype(jnp.bfloat16)
-    hot_back = hot.reshape(Z, plane * cap, tokens).transpose(0, 2, 1)
-    here = ids == me
-    taken = jnp.any(here, axis=1)
-    gate_here = jnp.sum(jnp.where(here, gates, 0.0), axis=1)
-    row_gate = jnp.sum(
-        jnp.where(
-            taken[:, None, :] & (places(taken)[:, None, :] == slots[None, :, None]),
-            gate_here[:, None, :],
-            0.0,
-        ),
-        axis=2,
-    ).reshape(experts * cap, 1)
-
-    attention = lax.psum_scatter(
-        attn_parts[0], "tensor", scatter_dimension=1, tiled=True
-    ).astype(jnp.float32)
-    hidden_in = resid.astype(jnp.float32) + attention
-    inv_rms = lax.rsqrt(row_sums(hidden_in * hidden_in) / D + epsilon)
-    normed = (hidden_in * inv_rms[:, None] * norm_gain[None, :]).astype(jnp.bfloat16)
-
-    arrived = dispatch(grad_out, normed, hot, plane, cap).reshape(2, experts * cap, width)
-    grad_rows, rows = arrived[0], arrived[1]
-    gate_part = jnp.dot(rows, w_gate[0], preferred_element_type=jnp.float32)
-    up_part = jnp.dot(rows, w_up[0], preferred_element_type=jnp.float32)
-    grad_part = jnp.dot(grad_rows, w_down[0].T, preferred_element_type=jnp.float32)
-    summed = lax.psum(
-        jnp.stack([gate_part, up_part, grad_part]).astype(jnp.bfloat16), "tensor"
-    ).astype(jnp.float32)
-    gate_pre, up_pre, grad_act = summed[0], summed[1], summed[2] * row_gate
-    sigmoid_gate = jax.nn.sigmoid(gate_pre)
-    swish = gate_pre * sigmoid_gate
-    activation = (swish * up_pre).astype(jnp.bfloat16)
-    expert_out = (
-        jnp.dot(activation, w_down[0], preferred_element_type=jnp.float32) * row_gate
-    ).astype(jnp.bfloat16)
-    grad_gate = grad_act * up_pre * sigmoid_gate * (1.0 + gate_pre * (1.0 - sigmoid_gate))
-    grad_up = grad_act * swish
-    grad_expert = (
-        jnp.dot(grad_gate.astype(jnp.bfloat16), w_gate[0].T, preferred_element_type=jnp.float32)
-        + jnp.dot(grad_up.astype(jnp.bfloat16), w_up[0].T, preferred_element_type=jnp.float32)
-    ).astype(jnp.bfloat16)
-    out_rows = jnp.stack([expert_out, grad_expert]).reshape(2, experts, cap, width)
-    sums = combine(out_rows, hot_back, tokens, plane)
+    inv_rms = inv[:, 0]
+    out_rows = expert_layer(
+        rows.reshape(2, experts * cap, width), w_gate[0], w_up[0], w_down[0]
+    ).reshape(2, experts, cap, width)
+    sums = combine(out_rows, hot, gate, tokens, plane)
     moe, grad_normed = sums[0], sums[1]
 
     output = (hidden_in + moe).astype(jnp.bfloat16)

time: 300 us -> 212 us (0.71)
  waiting for transfers between devices: 35.6 us -> 0 us
  Pallas kernels: 165 us -> 199 us
  blocking collectives: 37 us -> 3.58 us
  matrix products: 21.8 us -> 0 us
  between operations: 14.3 us -> 0.68 us
  other arithmetic: 17.6 us -> 4.02 us
  local copies, waits for them, and re-layouts: 7.65 us -> 4.11 us
    psum x1 -> x0, waiting for transfers between devices: 34.9 us -> none  [body(): lax.psum(jnp.stack([gate_part, up_part, grad_part]).astype(jnp.bfloat16),...]
    pallas_call x1 -> x2, Pallas kernels: 78.5 us -> 104 us  [the longest x1 75.2 us: dispatch(): pl.pallas_call(functools.partial(dispatch_kernel, plane), out_shape=(jax....]
    all_gather x1 -> x0, blocking collectives: 23.8 us -> none  [body(): lax.all_gather(jnp.concatenate([expert_ids.T.astype(jnp.float32), gate_we...]
    dot_general x8 -> x0, matrix products: 21.8 us -> none  [the longest x1 5.49 us: body(): jnp.dot(grad_up.astype(jnp.bfloat16), w_up[0].T, preferred_element_type=j...]
    psum x2 -> x1, blocking collectives: 13.2 us -> 3.58 us  [row_sums(): return lax.psum(jnp.sum(values, axis=1), 'tensor')]
    pallas_call x1, Pallas kernels: 86.8 us -> 94.8 us  [combine(): pl.pallas_call(functools.partial(combine_kernel, plane), out_shape=jax.Sh...]
    another operation x2 -> x0, other arithmetic: 5.23 us -> none  [the longest x1 3.2 us: body(): jnp.stack([expert_out, grad_expert]).reshape(2, experts, cap, width)]
    convert_element_type x3 -> x0, other arithmetic: 4.1 us -> none  [the longest x1 2.6 us: body(): summed = lax.psum(jnp.stack([gate_part, up_part, grad_part]).astype(jnp.b...]
  transfers between devices with their start and end apart: 2 -> 0, of which waited for: 1 -> 0; matrix products, arithmetic and copies ran while one was open for 2% -> 0% of each run, Pallas kernels for 0% -> 0%
where the time goes in v2:
time: 212 us; the launch traced here: 211 us
  Pallas kernels  199 us (94%)
  local copies, waits for them, and re-layouts  4.11 us (2%)
  other arithmetic  4.02 us (2%)
  blocking collectives  3.58 us (2%)
    pallas_call x1, Pallas kernels, combine(): pl.pallas_call(functools.partial(combine_kernel, plane), out_shape=jax.Sh...  94.8 us
    pallas_call x1, Pallas kernels, dispatch(): pl.pallas_call(functools.partial(dispatch_kernel, plane), out_shape=(jax....  75.2 us
    pallas_call x1, Pallas kernels, expert_layer(): pl.pallas_call(expert_kernel, out_shape=jax.ShapeDtypeStruct((2, total, w...  28.9 us

profile of v2, /device:TPU:17, one launch (start us, length us, event | category | flops | bytes accessed | tf_op | source)
XLA Modules:
  0.0 211.3 jit_solution(8133853947997247086)
XLA Ops:
  0.6 0.7 convert_bitcast_fusion
  1.3 0.7 pad_maximum_fusion.table_ref
  2.0 0.0 copy-start
  2.0 1.0 copy-done
  3.0 0.0 copy-start.1
  3.0 1.2 copy-done.1
  4.3 0.0 copy-start.2
  4.3 1.0 copy-done.2
  5.3 0.0 copy-start.3
  5.3 0.7 copy-done.3
  6.0 75.2 %shard_map.104 = (bf16[2,16,48,2048]{3,2,1,0:T(8,128)(2,1)}, f32[128,2048]{1,0:T(8,128)S(1)}, f32[128,128]{1,0:T(8,128)S(1)}, bf16[4,192,128]{2,1,0:T(8,128)(2,1)S(1)}, f32[4,192,128]{2,1,0:T(8,128)S(1)}) custom-call(bf16[128,4096]{1,0:T(8,128)(2,1)S(1)} %bitcast.20, bf16[128,2048]{1,0:T(8,128)(2,1)S(1)} %copy-done.2, f32[1,2048]{1,0:T(1,128)S(1)} %bitcast.21, ...), custom_call_target="tpu_custom_call" | custom-call | tf_op jit(solution)/shard_map/pallas_call | solution.py:550
  81.3 28.9 %shard_map.105 = bf16[2,768,2048]{2,1,0:T(8,128)(2,1)} custom-call(bf16[2,768,2048]{2,1,0:T(8,128)(2,1)} %bitcast.23, bf16[2048,768]{1,0:T(8,128)(2,1)} %bitcast.24, bf16[2048,768]{1,0:T(8,128)(2,1)} %bitcast.25, bf16[768,2048]{1,0:T(8,128)(2,1)} %bitcast.26), custom_call_target="tpu_custom_call" | custom-call | tf_op jit(solution)/shard_map/pallas_call | solution.py:531
  110.2 0.0 copy-start.4
  110.2 94.8 %shard_map.106 = f32[2,128,2048]{2,1,0:T(8,128)S(1)} custom-call(bf16[2,16,48,2048]{3,2,1,0:T(8,128)(2,1)} %bitcast.22, bf16[4,192,128]{2,1,0:T(8,128)(2,1)S(1)} %get-tuple-element.9.hot_ref, f32[4,192,128]{2,1,0:T(8,128)S(1)} %get-tuple-element.10.gate_ref), custom_call_target="tpu_custom_call" | custom-call | tf_op jit(solution)/shard_map/pallas_call | solution.py:585
  205.0 0.1 slice_reduce_fusion
  205.1 0.0 copy-done.4
  205.1 0.2 multiply_reduce_fusion
  205.3 3.6 %psum.7 = f32[128]{0:T(128)S(1)} all-reduce(f32[128]{0:T(128)S(1)} %multiply_reduce_fusion), channel_id=1, replica_groups=mesh['expert'=16,'tensor'=2] {'tensor'}, use_global_device_ids=true, to_apply=%region_1.0 | all-reduce | flops 128 | bytes 1024 | tf_op jit(solution)/shard_map/psum | solution.py:606
  208.9 2.4 %subtract_convert_fusion = (bf16[128,2048]{1,0:T(8,128)(2,1)}, bf16[128,2048]{1,0:T(8,128)(2,1)}) fusion(f32[128,2048]{1,0:T(8,128)S(1)} %get-tuple-element.7, bf16[128,2048]{1,0:T(8,128)(2,1)} %grad_ref.1, f32[2,128,2048]{2,1,0:T(8,128)S(1)} %shard_map.106, f32[128]{0:T(128)S(1)} %fusion.2, f32[2048]{0:T(1024)S(1)} %copy-done.4, f32[128]{0:T(128)S(1)} %slice_reduce_fusion), kind=kLoop, calls=%fused_computation.3 | loop fusion | flops 2359296 | bytes 4727808 | tf_op jit(solution)/shard_map/convert_element_type | solution.py:635
  (1 shorter events, 0.0 us)
Async XLA Ops:
  2.0 1.0 copy-start
  3.0 1.2 copy-start.1
  4.3 1.0 copy-start.2
  5.3 0.7 copy-start.3
  110.2 94.9 %copy-start.4 = (f32[2048]{0:T(1024)S(1)}, f32[2048]{0:T(1024)}, u32[]{:S(2)}) copy-start(f32[2048]{0:T(1024)} %param.11) | copy-start | bytes 24580

commit v3 on v2

--- a/solution.py
+++ b/solution.py
@@ -291,10 +291,102 @@
 
 
 def combine_kernel(
-    plane, out_rows, hot_ref, gate_ref, sum_ref, back, inc, leave, line_send, line_recv, send, recv
+    plane,
+    rows_ref,
+    w_gate,
+    w_up,
+    w_down,
+    hot_ref,
+    gate_ref,
+    sum_ref,
+    out_rows,
+    mine,
+    theirs,
+    back,
+    inc,
+    leave,
+    line_send,
+    line_recv,
+    send,
+    recv,
+    pair_send,
+    pair_recv,
 ):
     me, z, p = position(plane)
     cap, width = back.shape[3], back.shape[4]
+    last = (((1,), (1,)), ((), ()))
+
+    def pair_copy(c):
+        return pltpu.make_async_remote_copy(
+            src_ref=mine.at[c],
+            dst_ref=theirs.at[c],
+            send_sem=pair_send.at[c],
+            recv_sem=pair_recv.at[c],
+            device_id=partner(),
+            device_id_type=MESH,
+        )
+
+    def first_half(c):
+        rows = rows_ref[1, c]
+        mine[c, 0] = jnp.dot(rows, w_gate[...], preferred_element_type=jnp.float32).astype(
+            jnp.bfloat16
+        )
+        mine[c, 1] = jnp.dot(rows, w_up[...], preferred_element_type=jnp.float32).astype(
+            jnp.bfloat16
+        )
+        mine[c, 2] = lax.dot_general(
+            rows_ref[0, c], w_down[...], last, preferred_element_type=jnp.float32
+        ).astype(jnp.bfloat16)
+        pair_copy(c).start()
+
+    def second_half(c):
+        pair_copy(c).wait()
+        gate_pre, up_pre, grad_act = (
+            mine[c, i].astype(jnp.float32) + theirs[c, i].astype(jnp.float32) for i in range(3)
+        )
+        sigmoid_gate = 1.0 / (1.0 + jnp.exp(-gate_pre))
+        swish = gate_pre * sigmoid_gate
+        mine[c, 0] = (swish * up_pre).astype(jnp.bfloat16)
+        mine[c, 1] = (
+            grad_act * up_pre * sigmoid_gate * (1.0 + gate_pre * (1.0 - sigmoid_gate))
+        ).astype(jnp.bfloat16)
+        mine[c, 2] = (grad_act * swish).astype(jnp.bfloat16)
+        groups = pl.ds(c * plane, plane)
+
+        def down(i, inner):
+            columns = pl.ds(pl.multiple_of(i * COLUMNS, COLUMNS), COLUMNS)
+            out_rows[0, groups, :, columns] = (
+                jnp.dot(mine[c, 0], w_down[:, columns], preferred_element_type=jnp.float32)
+                .astype(jnp.bfloat16)
+                .reshape(plane, cap, COLUMNS)
+            )
+            return inner
+
+        def up(i, inner):
+            columns = pl.ds(pl.multiple_of(i * COLUMNS, COLUMNS), COLUMNS)
+            out_rows[1, groups, :, columns] = (
+                (
+                    lax.dot_general(
+                        mine[c, 1], w_gate[columns, :], last, preferred_element_type=jnp.float32
+                    )
+                    + lax.dot_general(
+                        mine[c, 2], w_up[columns, :], last, preferred_element_type=jnp.float32
+                    )
+                )
+                .astype(jnp.bfloat16)
+                .reshape(plane, cap, COLUMNS)
+            )
+            return inner
+
+        lax.fori_loop(0, width // COLUMNS, down, 0)
+        post(0, c)
+        lax.fori_loop(0, width // COLUMNS, up, 0)
+        post(1, c)
+
+    def order(i):
+        falling = Z - 1 - i - jnp.where(Z - 1 - i <= z, 1, 0)
+        rising = i + jnp.where(i >= z, 1, 0)
+        return jnp.where(i == Z - 1, z, jnp.where(z < Z // 2, falling, rising))
 
     def plane_copy(a, origin, q, sender):
         return pltpu.make_async_remote_copy(
@@ -312,7 +404,7 @@
             dst_ref=inc.at[a, way, origin],
             send_sem=line_send.at[a, origin],
             recv_sem=line_recv.at[a, way, origin],
-            device_id=device(me + plane if way == 0 else me - plane),
+            device_id=device(me + plane - 2 * plane * way),
             device_id_type=MESH,
         )
 
@@ -353,62 +445,49 @@
             high, rows, first, preferred_element_type=jnp.float32
         ) + lax.dot_general(low, rows, first, preferred_element_type=jnp.float32)
 
-    greet(plane, False)
+    def line_step(origin):
+        way = jnp.where(origin > z, 0, 1)
+        comes_here = jnp.where(way == 0, z, Z - 1 - z) > 0
+        for a in range(2):
+            gather(a, origin)
+
+            @pl.when(comes_here)
+            def _(a=a):
+                line_copy(a, way, origin).wait_recv()
+
+                @each_chunk
+                def _(columns):
+                    earlier = inc[a, way, origin, :, columns].astype(jnp.float32)
+                    leave[a, origin, :, columns] = (
+                        partial(a, origin, columns) + earlier
+                    ).astype(jnp.bfloat16)
+
+            @pl.when(jnp.logical_not(comes_here))
+            def _(a=a):
+                @each_chunk
+                def _(columns):
+                    leave[a, origin, :, columns] = partial(a, origin, columns).astype(jnp.bfloat16)
+
+            line_copy(a, way, origin).start()
+
+    greet(plane, True)
     comes = (z > 0, z < Z - 1)
-
-    def far(way, step):
-        origin = z + step if way == 0 else z - step
-        return origin, (z + step < Z if way == 0 else z >= step)
-
-    for step in range(Z - 1, 0, -1):
-        for a in range(2):
-            for way in range(2):
-                origin, there = far(way, step)
-
-                @pl.when(there)
-                def _(a=a, origin=origin):
-                    post(a, origin)
-
-    for a in range(2):
-        post(a, z)
-
-    for step in range(Z - 1, 0, -1):
-        for a in range(2):
-            for way in range(2):
-                origin, there = far(way, step)
-
-                @pl.when(there)
-                def _(a=a, way=way, step=step, origin=origin):
-                    gather(a, origin)
-                    if step == Z - 1:
-
-                        @each_chunk
-                        def _(columns):
-                            leave[a, origin, :, columns] = partial(a, origin, columns).astype(
-                                jnp.bfloat16
-                            )
-                    else:
-
-                        @pl.when(comes[way])
-                        def _():
-                            line_copy(a, way, origin).wait_recv()
-
-                            @each_chunk
-                            def _(columns):
-                                earlier = inc[a, way, origin, :, columns].astype(jnp.float32)
-                                leave[a, origin, :, columns] = (
-                                    partial(a, origin, columns) + earlier
-                                ).astype(jnp.bfloat16)
-
-                        @pl.when(jnp.logical_not(comes[way]))
-                        def _():
-                            @each_chunk
-                            def _(columns):
-                                leave[a, origin, :, columns] = partial(a, origin, columns).astype(
-                                    jnp.bfloat16
-                                )
-
-                    line_copy(a, way, origin).start()
+    first_half(order(0))
+
+    def work(i, carry):
+        @pl.when(i + 1 < Z)
+        def _():
+            first_half(order(i + 1))
+
+        second_half(order(i))
+
+        @pl.when(i > 0)
+        def _():
+            line_step(order(i - 1))
+
+        return carry
+
+    lax.fori_loop(0, Z, work, 0)
 
     for a in range(2):
         gather(a, z)
@@ -428,14 +507,10 @@
                 def _(columns):
                     sum_ref[a, :, columns] += inc[a, way, z, :, columns].astype(jnp.float32)
 
-    for step in range(Z - 1, 0, -1):
+    for i in range(Z - 1):
+        origin = order(i)
         for a in range(2):
-            for way in range(2):
-                origin, there = far(way, step)
-
-                @pl.when(there)
-                def _(a=a, way=way, origin=origin):
-                    line_copy(a, way, origin).wait_send()
+            line_copy(a, jnp.where(origin > z, 0, 1), origin).wait_send()
 
     def finish(i, carry):
         a, origin, d = i // (Z * plane), (i // plane) % Z, i % plane
@@ -450,99 +525,6 @@
 
 
 VM = pl.BlockSpec(memory_space=pltpu.VMEM)
-
-
-def expert_kernel(
-    rows_ref, gate_ref, up_ref, down_ref, out_ref, mine, theirs, send, recv
-):
-    count, part = mine.shape[0], mine.shape[2]
-    width = rows_ref.shape[2]
-    last = (((1,), (1,)), ((), ()))
-    barrier = pltpu.get_barrier_semaphore()
-    pl.semaphore_signal(barrier, inc=1, device_id=partner(), device_id_type=MESH)
-    pl.semaphore_wait(barrier, 1)
-
-    def copy(c):
-        return pltpu.make_async_remote_copy(
-            src_ref=mine.at[c],
-            dst_ref=theirs.at[c],
-            send_sem=send.at[c],
-            recv_sem=recv.at[c],
-            device_id=partner(),
-            device_id_type=MESH,
-        )
-
-    def first_half(c, carry):
-        at = pl.ds(pl.multiple_of(c * part, part), part)
-        rows = rows_ref[1, at, :]
-        mine[c, 0] = jnp.dot(rows, gate_ref[...], preferred_element_type=jnp.float32).astype(
-            jnp.bfloat16
-        )
-        mine[c, 1] = jnp.dot(rows, up_ref[...], preferred_element_type=jnp.float32).astype(
-            jnp.bfloat16
-        )
-        mine[c, 2] = lax.dot_general(
-            rows_ref[0, at, :], down_ref[...], last, preferred_element_type=jnp.float32
-        ).astype(jnp.bfloat16)
-        copy(c).start()
-        return carry
-
-    def second_half(c, carry):
-        at = pl.ds(pl.multiple_of(c * part, part), part)
-        copy(c).wait()
-        gate_pre, up_pre, grad_act = (
-            mine[c, i].astype(jnp.float32) + theirs[c, i].astype(jnp.float32) for i in range(3)
-        )
-        sigmoid_gate = 1.0 / (1.0 + jnp.exp(-gate_pre))
-        swish = gate_pre * sigmoid_gate
-        mine[c, 0] = (swish * up_pre).astype(jnp.bfloat16)
-        mine[c, 1] = (
-            grad_act * up_pre * sigmoid_gate * (1.0 + gate_pre * (1.0 - sigmoid_gate))
-        ).astype(jnp.bfloat16)
-        mine[c, 2] = (grad_act * swish).astype(jnp.bfloat16)
-
-        def chunk(i, inner):
-            columns = pl.ds(pl.multiple_of(i * COLUMNS, COLUMNS), COLUMNS)
-            out_ref[0, at, columns] = jnp.dot(
-                mine[c, 0], down_ref[:, columns], preferred_element_type=jnp.float32
-            ).astype(jnp.bfloat16)
-            out_ref[1, at, columns] = (
-                lax.dot_general(
-                    mine[c, 1], gate_ref[columns, :], last, preferred_element_type=jnp.float32
-                )
-                + lax.dot_general(
-                    mine[c, 2], up_ref[columns, :], last, preferred_element_type=jnp.float32
-                )
-            ).astype(jnp.bfloat16)
-            return inner
-
-        lax.fori_loop(0, width // COLUMNS, chunk, 0)
-        return carry
-
-    lax.fori_loop(0, count, first_half, 0)
-    lax.fori_loop(0, count, second_half, 0)
-
-
-def expert_layer(rows, w_gate, w_up, w_down):
-    _, total, width = rows.shape
-    hidden = w_gate.shape[1]
-    part = 256
-    count = total // part
-    return pl.pallas_call(
-        expert_kernel,
-        out_shape=jax.ShapeDtypeStruct((2, total, width), jnp.bfloat16),
-        in_specs=[VM] * 4,
-        out_specs=VM,
-        scratch_shapes=[
-            pltpu.VMEM((count, 3, part, hidden), jnp.bfloat16),
-            pltpu.VMEM((count, 3, part, hidden), jnp.bfloat16),
-            pltpu.SemaphoreType.DMA((count,)),
-            pltpu.SemaphoreType.DMA((count,)),
-        ],
-        compiler_params=pltpu.CompilerParams(
-            collective_id=2, has_side_effects=True, vmem_limit_bytes=52 << 20
-        ),
-    )(rows, w_gate, w_up, w_down)
 
 
 def dispatch(attn, resid, gain, grad_out, table, plane, cap):
@@ -580,14 +562,18 @@
     )(attn, resid, gain, grad_out, table)
 
 
-def combine(out_rows, hot, gate, tokens, plane):
-    _, _, cap, width = out_rows.shape
+def combine(rows, w_gate, w_up, w_down, hot, gate, tokens, plane):
+    _, groups, cap, width = rows.shape
+    hidden = w_gate.shape[1]
     return pl.pallas_call(
         functools.partial(combine_kernel, plane),
         out_shape=jax.ShapeDtypeStruct((2, tokens, width), jnp.float32),
-        in_specs=[VM] * 3,
+        in_specs=[VM] * 6,
         out_specs=VM,
         scratch_shapes=[
+            pltpu.VMEM((2, groups, cap, width), jnp.bfloat16),
+            pltpu.VMEM((Z, 3, plane * cap, hidden), jnp.bfloat16),
+            pltpu.VMEM((Z, 3, plane * cap, hidden), jnp.bfloat16),
             pltpu.VMEM((2, Z, plane, cap, width), jnp.bfloat16),
             pltpu.VMEM((2, 2, Z, tokens, width), jnp.bfloat16),
             pltpu.VMEM((2, Z, tokens, width), jnp.bfloat16),
@@ -595,11 +581,13 @@
             pltpu.SemaphoreType.DMA((2, 2, Z)),
             pltpu.SemaphoreType.DMA((2, Z, plane)),
             pltpu.SemaphoreType.DMA((2, Z, plane)),
+            pltpu.SemaphoreType.DMA((Z,)),
+            pltpu.SemaphoreType.DMA((Z,)),
         ],
         compiler_params=pltpu.CompilerParams(
-            collective_id=1, has_side_effects=True, vmem_limit_bytes=48 << 20
+            collective_id=1, has_side_effects=True, vmem_limit_bytes=62 << 20
         ),
-    )(out_rows, hot, gate)
+    )(rows.reshape(2, Z, plane * cap, width), w_gate, w_up, w_down, hot, gate)
 
 
 def row_sums(values):
@@ -618,10 +606,7 @@
         attn_parts[0], resid, norm_gain[None, :], grad_out, table, plane, cap
     )
     inv_rms = inv[:, 0]
-    out_rows = expert_layer(
-        rows.reshape(2, experts * cap, width), w_gate[0], w_up[0], w_down[0]
-    ).reshape(2, experts, cap, width)
-    sums = combine(out_rows, hot, gate, tokens, plane)
+    sums = combine(rows, w_gate[0], w_up[0], w_down[0], hot, gate, tokens, plane)
     moe, grad_normed = sums[0], sums[1]
 
     output = (hidden_in + moe).astype(jnp.bfloat16)

time: 212 us -> 208 us (0.981); the launches traced: 211 us -> 204 us
  Pallas kernels: 199 us -> 187 us
    pallas_call x1 -> x0, Pallas kernels: 28.9 us -> none  [expert_layer(): pl.pallas_call(expert_kernel, out_shape=jax.ShapeDtypeStruct((2, total, w...]
    pallas_call x1, Pallas kernels: 94.8 us -> 112 us  [combine(): pl.pallas_call(functools.partial(combine_kernel, plane), out_shape=jax.Sh...]
    unnamed x10 -> x16, local copies, waits for them, and re-layouts: 4.01 us -> 5.43 us
where the time goes in v3:
time: 208 us; the launch traced here: 204 us
  Pallas kernels  187 us (90%)
  other arithmetic  5.74 us (3%)
  local copies, waits for them, and re-layouts  5.53 us (3%)
  blocking collectives  5.13 us (2%)
    pallas_call x1, Pallas kernels, combine(): pl.pallas_call(functools.partial(combine_kernel, plane), out_shape=jax.Sh...  112 us
    pallas_call x1, Pallas kernels, dispatch(): pl.pallas_call(functools.partial(dispatch_kernel, plane), out_shape=(jax....  75.2 us
    unnamed x16, local copies, waits for them, and re-layouts  5.43 us
    psum x1, blocking collectives, row_sums(): return lax.psum(jnp.sum(values, axis=1), 'tensor')  5.13 us

profile of v3, /device:TPU:17, one launch (start us, length us, event | category | flops | bytes accessed | tf_op | source)
XLA Modules:
  0.0 203.9 jit_solution(9288591392109067509)
XLA Ops:
  0.6 0.7 convert_bitcast_fusion
  1.3 0.7 pad_maximum_fusion.table_ref
  2.0 0.0 copy-start
  2.0 1.0 copy-done
  3.0 0.0 copy-start.2
  3.0 1.2 copy-done.2
  4.3 0.0 copy-start.3
  4.3 1.0 copy-done.3
  5.3 0.0 copy-start.6
  5.3 0.7 copy-done.6
  6.0 75.2 %shard_map.104 = (bf16[2,16,48,2048]{3,2,1,0:T(8,128)(2,1)}, f32[128,2048]{1,0:T(8,128)S(1)}, f32[128,128]{1,0:T(8,128)S(1)}, bf16[4,192,128]{2,1,0:T(8,128)(2,1)S(1)}, f32[4,192,128]{2,1,0:T(8,128)S(1)}) custom-call(bf16[128,4096]{1,0:T(8,128)(2,1)S(1)} %bitcast.19, bf16[128,2048]{1,0:T(8,128)(2,1)S(1)} %copy-done.3, f32[1,2048]{1,0:T(1,128)S(1)} %bitcast.20, ...), custom_call_target="tpu_custom_call" | custom-call | tf_op jit(solution)/shard_map/pallas_call | solution.py:532
  81.2 0.0 copy-start.4
  81.3 0.7 copy-done.4
  82.0 0.0 copy-start.5
  82.0 0.7 copy-done.5
  82.7 0.0 copy-start.7
  82.7 0.0 copy-start.1
  82.7 111.6 %shard_map.105 = f32[2,128,2048]{2,1,0:T(8,128)} custom-call(bf16[2,4,192,2048]{3,2,1,0:T(8,128)(2,1)} %bitcast.21, bf16[2048,768]{1,0:T(8,128)(2,1)} %bitcast.22, bf16[2048,768]{1,0:T(8,128)(2,1)} %bitcast.23, bf16[768,2048]{1,0:T(8,128)(2,1)} %bitcast.24, bf16[4,192,128]{2,1,0:T(8,128)(2,1)} %copy-done.5, f32[4,192,128]{2,1,0:T(8,128)} %copy-done.4), custom_call_target="tpu_custom_call" | custom-call | tf_op jit(solution)/shard_map/pallas_call | solution.py:568
  194.3 0.1 slice_reduce_fusion
  194.4 0.0 copy-done.7
  194.4 1.4 multiply_reduce_fusion
  195.8 5.1 %psum.7 = f32[128]{0:T(128)S(1)} all-reduce(f32[128]{0:T(128)S(1)} %multiply_reduce_fusion), channel_id=1, replica_groups=mesh['expert'=16,'tensor'=2] {'tensor'}, use_global_device_ids=true, to_apply=%region_1.0 | all-reduce | flops 128 | bytes 1024 | tf_op jit(solution)/shard_map/psum | solution.py:594
  201.0 0.0 copy-done.1
  201.0 2.9 %subtract_convert_fusion = (bf16[128,2048]{1,0:T(8,128)(2,1)}, bf16[128,2048]{1,0:T(8,128)(2,1)}) fusion(f32[128,2048]{1,0:T(8,128)S(1)} %get-tuple-element.7, bf16[128,2048]{1,0:T(8,128)(2,1)S(1)} %copy-done.1, f32[2,128,2048]{2,1,0:T(8,128)} %shard_map.105, f32[128]{0:T(128)S(1)} %fusion.2, f32[2048]{0:T(1024)S(1)} %copy-done.7, f32[128]{0:T(128)S(1)} %slice_reduce_fusion), kind=kLoop, calls=%fused_computation.3 | loop fusion | flops 2359296 | bytes 4727808 | tf_op jit(solution)/shard_map/convert_element_type | solution.py:620
  (1 shorter events, 0.0 us)
Async XLA Ops:
  2.0 1.0 copy-start
  3.0 1.2 copy-start.2
  4.3 1.0 copy-start.3
  5.3 0.7 copy-start.6
  81.2 0.7 copy-start.4
  82.0 0.7 copy-start.5
  82.7 111.7 %copy-start.7 = (f32[2048]{0:T(1024)S(1)}, f32[2048]{0:T(1024)}, u32[]{:S(2)}) copy-start(f32[2048]{0:T(1024)} %param.11) | copy-start | bytes 24580
  82.7 118.3 %copy-start.1 = (bf16[128,2048]{1,0:T(8,128)(2,1)S(1)}, bf16[128,2048]{1,0:T(8,128)(2,1)}, u32[]{:S(2)}) copy-start(bf16[128,2048]{1,0:T(8,128)(2,1)} %grad_ref.1) | copy-start | bytes 1572868

commit v4 on v3

--- a/solution.py
+++ b/solution.py
@@ -298,7 +298,14 @@
     w_down,
     hot_ref,
     gate_ref,
+    hidden_ref,
+    inv_ref,
+    gain_ref,
+    grad_ref,
+    output_ref,
+    input_ref,
     sum_ref,
+    stat,
     out_rows,
     mine,
     theirs,
@@ -398,10 +405,13 @@
             device_id_type=MESH,
         )
 
-    def line_copy(a, way, origin):
+    def place(way, origin, at):
+        return jnp.where(origin == at, origin + (Z - origin) * way, origin)
+
+    def line_copy(a, way, origin, at):
         return pltpu.make_async_remote_copy(
             src_ref=leave.at[a, origin],
-            dst_ref=inc.at[a, way, origin],
+            dst_ref=inc.at[a, place(way, origin, at)],
             send_sem=line_send.at[a, origin],
             recv_sem=line_recv.at[a, way, origin],
             device_id=device(me + plane - 2 * plane * way),
@@ -453,11 +463,11 @@
 
             @pl.when(comes_here)
             def _(a=a):
-                line_copy(a, way, origin).wait_recv()
+                line_copy(a, way, origin, z).wait_recv()
 
                 @each_chunk
                 def _(columns):
-                    earlier = inc[a, way, origin, :, columns].astype(jnp.float32)
+                    earlier = inc[a, origin, :, columns].astype(jnp.float32)
                     leave[a, origin, :, columns] = (
                         partial(a, origin, columns) + earlier
                     ).astype(jnp.bfloat16)
@@ -468,19 +478,19 @@
                 def _(columns):
                     leave[a, origin, :, columns] = partial(a, origin, columns).astype(jnp.bfloat16)
 
-            line_copy(a, way, origin).start()
+            line_copy(a, way, origin, z + 1 - 2 * way).start()
 
     greet(plane, True)
     comes = (z > 0, z < Z - 1)
     first_half(order(0))
 
     def work(i, carry):
+        second_half(order(i))
+
         @pl.when(i + 1 < Z)
         def _():
             first_half(order(i + 1))
 
-        second_half(order(i))
-
         @pl.when(i > 0)
         def _():
             line_step(order(i - 1))
@@ -501,16 +511,53 @@
 
             @pl.when(comes[way])
             def _(a=a, way=way):
-                line_copy(a, way, z).wait_recv()
+                line_copy(a, way, z, z).wait_recv()
 
                 @each_chunk
                 def _(columns):
-                    sum_ref[a, :, columns] += inc[a, way, z, :, columns].astype(jnp.float32)
+                    sum_ref[a, :, columns] += inc[a, z if way == 0 else Z, :, columns].astype(jnp.float32)
+
+    stat_copy = pltpu.make_async_remote_copy(
+        src_ref=stat.at[0],
+        dst_ref=stat.at[1],
+        send_sem=pair_send.at[Z],
+        recv_sem=pair_recv.at[Z],
+        device_id=partner(),
+        device_id_type=MESH,
+    )
+    stat[0] = jnp.zeros(inv_ref.shape, jnp.float32)
+
+    @each_chunk
+    def _(columns):
+        scaled = sum_ref[1, :, columns] * gain_ref[:, columns]
+        sum_ref[1, :, columns] = scaled
+        inner = jnp.sum(hidden_ref[:, columns] * scaled, axis=1, keepdims=True)
+        stat[0] += jnp.broadcast_to(inner, inv_ref.shape)
+
+    stat_copy.start()
+
+    @each_chunk
+    def _(columns):
+        output_ref[:, columns] = (hidden_ref[:, columns] + sum_ref[0, :, columns]).astype(
+            jnp.bfloat16
+        )
+
+    stat_copy.wait()
+    inv_rms = inv_ref[...]
+    stat[0] = inv_rms * inv_rms * inv_rms * (stat[0] + stat[1]) / D
+
+    @each_chunk
+    def _(columns):
+        input_ref[:, columns] = (
+            grad_ref[:, columns].astype(jnp.float32)
+            + inv_ref[:, 0:1] * sum_ref[1, :, columns]
+            - hidden_ref[:, columns] * stat[0, :, 0:1]
+        ).astype(jnp.bfloat16)
 
     for i in range(Z - 1):
         origin = order(i)
         for a in range(2):
-            line_copy(a, jnp.where(origin > z, 0, 1), origin).wait_send()
+            line_copy(a, jnp.where(origin > z, 0, 1), origin, z).wait_send()
 
     def finish(i, carry):
         a, origin, d = i // (Z * plane), (i // plane) % Z, i % plane
@@ -562,36 +609,35 @@
     )(attn, resid, gain, grad_out, table)
 
 
-def combine(rows, w_gate, w_up, w_down, hot, gate, tokens, plane):
+def combine(rows, w_gate, w_up, w_down, hot, gate, hidden_in, inv, gain, grad_out, plane):
     _, groups, cap, width = rows.shape
     hidden = w_gate.shape[1]
+    tokens = grad_out.shape[0]
     return pl.pallas_call(
         functools.partial(combine_kernel, plane),
-        out_shape=jax.ShapeDtypeStruct((2, tokens, width), jnp.float32),
-        in_specs=[VM] * 6,
-        out_specs=VM,
+        out_shape=(jax.ShapeDtypeStruct((tokens, width), jnp.bfloat16),) * 2,
+        in_specs=[VM] * 10,
+        out_specs=(VM,) * 2,
         scratch_shapes=[
+            pltpu.VMEM((2, tokens, width), jnp.float32),
+            pltpu.VMEM((2, tokens, 128), jnp.float32),
             pltpu.VMEM((2, groups, cap, width), jnp.bfloat16),
             pltpu.VMEM((Z, 3, plane * cap, hidden), jnp.bfloat16),
             pltpu.VMEM((Z, 3, plane * cap, hidden), jnp.bfloat16),
             pltpu.VMEM((2, Z, plane, cap, width), jnp.bfloat16),
-            pltpu.VMEM((2, 2, Z, tokens, width), jnp.bfloat16),
+            pltpu.VMEM((2, Z + 1, tokens, width), jnp.bfloat16),
             pltpu.VMEM((2, Z, tokens, width), jnp.bfloat16),
             pltpu.SemaphoreType.DMA((2, Z)),
             pltpu.SemaphoreType.DMA((2, 2, Z)),
             pltpu.SemaphoreType.DMA((2, Z, plane)),
             pltpu.SemaphoreType.DMA((2, Z, plane)),
-            pltpu.SemaphoreType.DMA((Z,)),
-            pltpu.SemaphoreType.DMA((Z,)),
+            pltpu.SemaphoreType.DMA((Z + 1,)),
+            pltpu.SemaphoreType.DMA((Z + 1,)),
         ],
         compiler_params=pltpu.CompilerParams(
             collective_id=1, has_side_effects=True, vmem_limit_bytes=62 << 20
         ),
-    )(rows.reshape(2, Z, plane * cap, width), w_gate, w_up, w_down, hot, gate)
-
-
-def row_sums(values):
-    return lax.psum(jnp.sum(values, axis=1), "tensor")
+    )(rows.reshape(2, Z, plane * cap, width), w_gate, w_up, w_down, hot, gate, hidden_in, inv, gain, grad_out)
 
 
 def body(attn_parts, resid, norm_gain, w_gate, w_up, w_down, expert_ids, gate_weights, grad_out):
@@ -605,19 +651,19 @@
     rows, hidden_in, inv, hot, gate = dispatch(
         attn_parts[0], resid, norm_gain[None, :], grad_out, table, plane, cap
     )
-    inv_rms = inv[:, 0]
-    sums = combine(rows, w_gate[0], w_up[0], w_down[0], hot, gate, tokens, plane)
-    moe, grad_normed = sums[0], sums[1]
-
-    output = (hidden_in + moe).astype(jnp.bfloat16)
-    scaled = grad_normed * norm_gain[None, :]
-    inner = row_sums(hidden_in * scaled)
-    grad_input = (
-        grad_out.astype(jnp.float32)
-        + inv_rms[:, None] * scaled
-        - hidden_in * (inv_rms**3 * inner / D)[:, None]
+    return combine(
+        rows,
+        w_gate[0],
+        w_up[0],
+        w_down[0],
+        hot,
+        gate,
+        hidden_in,
+        inv,
+        norm_gain[None, :],
+        grad_out,
+        plane,
     )
-    return (output, grad_input.astype(jnp.bfloat16))
 
 
 def solution(mesh):

time: 208 us -> 212 us (1.019)
  the two profiles are of different devices: /device:TPU:17 before, /device:TPU:0 now
where the time goes in v4:
time: 212 us
  Pallas kernels  199 us (94%)
  local copies, waits for them, and re-layouts  10.8 us (5%)
    pallas_call x1, Pallas kernels, combine(): pl.pallas_call(functools.partial(combine_kernel, plane), out_shape=(jax.S...  112 us
    pallas_call x1, Pallas kernels, dispatch(): pl.pallas_call(functools.partial(dispatch_kernel, plane), out_shape=(jax....  86.9 us
    unnamed x18, local copies, waits for them, and re-layouts  10.8 us

profile of v4, /device:TPU:0, one launch (start us, length us, event | category | flops | bytes accessed | tf_op | source)
XLA Modules:
  0.0 211.9 jit_solution(14053642449956862087)
XLA Ops:
  0.6 0.7 convert_bitcast_fusion
  1.3 0.7 pad_maximum_fusion.table_ref
  2.0 0.0 copy-start
  2.0 1.0 copy-done
  3.0 0.0 copy-start.2
  3.0 1.2 copy-done.2
  4.3 0.0 copy-start.3
  4.3 1.0 copy-done.3
  5.3 0.0 copy-start.7
  5.3 0.7 copy-done.7
  6.0 86.9 %shard_map.104 = (bf16[2,16,48,2048]{3,2,1,0:T(8,128)(2,1)}, f32[128,2048]{1,0:T(8,128)S(1)}, f32[128,128]{1,0:T(8,128)S(1)}, bf16[4,192,128]{2,1,0:T(8,128)(2,1)S(1)}, f32[4,192,128]{2,1,0:T(8,128)S(1)}) custom-call(bf16[128,4096]{1,0:T(8,128)(2,1)S(1)} %bitcast.9, bf16[128,2048]{1,0:T(8,128)(2,1)S(1)} %copy-done.3, f32[1,2048]{1,0:T(1,128)S(1)} %bitcast.11, ...), custom_call_target="tpu_custom_call" | custom-call | tf_op jit(solution)/shard_map/pallas_call | solution.py:579
  92.9 0.0 copy-start.1
  92.9 1.0 copy-done.1
  93.9 0.0 copy-start.4
  93.9 0.7 copy-done.4
  94.6 0.0 copy-start.5
  94.6 0.7 copy-done.5
  95.3 0.0 copy-start.6
  95.3 0.6 copy-done.6
  95.9 112.2 %shard_map.105 = (bf16[128,2048]{1,0:T(8,128)(2,1)}, bf16[128,2048]{1,0:T(8,128)(2,1)}) custom-call(bf16[2,4,192,2048]{3,2,1,0:T(8,128)(2,1)} %bitcast.12, bf16[2048,768]{1,0:T(8,128)(2,1)} %bitcast.13, bf16[2048,768]{1,0:T(8,128)(2,1)} %bitcast.14, bf16[768,2048]{1,0:T(8,128)(2,1)} %bitcast.15, bf16[4,192,128]{2,1,0:T(8,128)(2,1)} %copy-done.5, ...), custom_call_target="tpu_custom_call" | custom-call | tf_op jit(solution)/shard_map/pallas_call | solution.py:616
  208.1 1.9 copy.13
  210.0 1.9 copy.14
Async XLA Ops:
  2.0 1.0 copy-start
  3.0 1.2 copy-start.2
  4.3 1.0 copy-start.3
  5.3 0.7 copy-start.7
  92.9 1.0 copy-start.1
  93.9 0.7 copy-start.4
  94.6 0.7 copy-start.5
  95.3 0.6 copy-start.6
